TPU v7x, 32 devices: a whole 2x2x4 slice. The times are simulated.
32 devices in a mesh: seq: 8 (over z, y), tp: 4 (over x, core).
Axes of the slice: x: 2, y: 2, z: 4, core: 2. Of those that a mesh axis runs over, the one named last changes fastest.
Arguments:
- subsampled: bfloat16 [2048, 4096], P('seq'), may hold values from -6 to 6
- proj_weight: bfloat16 [4096, 1024], P(None, 'tp'), may hold values from -0.09375 to 0.09375
- value_weight: bfloat16 [1024, 1024], P(None, 'tp'), may hold values from -0.1875 to 0.1875
- gate_weight: bfloat16 [1024, 1024], P(None, 'tp'), may hold values from -0.1875 to 0.1875
- conv_kernel: float32 [9, 1024], P(None, 'tp'), may hold values from -2 to 2
- bn_gain: float32 [1024], P('tp'), may hold values from 0.5 to 1.5
- bn_shift: float32 [1024], P('tp'), may hold values from -2 to 2
- down_weight: bfloat16 [1024, 1024], P(None, 'tp'), may hold values from -0.1875 to 0.1875
- clip_frames: int32 [8, 8], replicated, may hold values from 1 to 64, 256 in all within a row
- clip_dest: int32 [8, 8], replicated, may hold values from 0 to 7, each once within a row
- out_grad: bfloat16 [4096, 1024], P('seq', 'tp'), may hold values from -0.13183594 to 0.13183594
Outputs:
- block_out: bfloat16 [4096, 1024], P('seq', 'tp')
- proj_grad: float32 [4096, 1024], P('seq', 'tp')
- value_grad: float32 [1024, 1024], P('seq', 'tp')
- gate_grad: float32 [1024, 1024], P('seq', 'tp')
- down_grad: float32 [1024, 1024], P('seq', 'tp')
- bn_gain_grad: float32 [1024], P('tp')
- bn_shift_grad: float32 [1024], P('tp')
Inputs may be any that keep to these rules, and one draw needn't show every extreme that they name: `clip_frames`: row s holds the frame counts of the 8 clips of owner s, summing to 256; the largest of each row is 64. `clip_dest`: each row is a permutation: owner s sends exactly one clip to every packed shard.
All inputs are finite; a program needn't handle non-finite values.
Results may differ from a plain program's by a relative error of at most 0.0077.
Values may be sent and summed in bfloat16 or wider, within the bound.
A program may use at most 192 MiB of HBM per device.

v0:
```python
import jax
import jax.numpy as jnp
from jax import lax
from jax.sharding import PartitionSpec as P

MOST = 64


def depthwise(field, kernel):
    half = kernel.shape[0] // 2
    length = field.shape[1]
    padded = jnp.pad(field, ((0, 0), (half, half), (0, 0)))
    total = jnp.zeros(field.shape, jnp.float32)
    for offset in range(kernel.shape[0]):
        total = total + kernel[offset] * padded[:, offset : offset + length]
    return total


def depthwise_back(grad, kernel):
    half = kernel.shape[0] // 2
    length = grad.shape[1]
    padded = jnp.pad(grad, ((0, 0), (half, half), (0, 0)))
    total = jnp.zeros(grad.shape, jnp.float32)
    for offset in range(kernel.shape[0]):
        begin = 2 * half - offset
        total = total + kernel[offset] * padded[:, begin : begin + length]
    return total


def contract_rows(left, right):
    return lax.dot_general(
        left, right, (((0,), (0,)), ((), ())), preferred_element_type=jnp.float32
    )


def contract_cols(left, right):
    return lax.dot_general(
        left, right, (((1,), (1,)), ((), ())), preferred_element_type=jnp.float32
    )


def body(
    subsampled,
    proj_weight,
    value_weight,
    gate_weight,
    conv_kernel,
    bn_gain,
    bn_shift,
    down_weight,
    clip_frames,
    clip_dest,
    out_grad,
):
    shards = lax.axis_size("seq")
    seq_index = lax.axis_index("seq")
    tp_index = lax.axis_index("tp")
    own_rows = subsampled.shape[0]
    part_width = proj_weight.shape[1]
    count = float(own_rows * shards)
    clip_lens = lax.dynamic_slice_in_dim(clip_frames, seq_index, 1, 0)[0]
    clip_targets = lax.dynamic_slice_in_dim(clip_dest, seq_index, 1, 0)[0]
    offsets = jnp.cumsum(clip_lens) - clip_lens
    shard_ids = jnp.arange(shards, dtype=jnp.int32)
    match = clip_targets[None, :] == shard_ids[:, None]
    starts = jnp.sum(jnp.where(match, offsets[None, :], 0), axis=1)
    lengths = jnp.sum(jnp.where(match, clip_lens[None, :], 0), axis=1)
    frame_pos = jnp.arange(MOST, dtype=jnp.int32)
    source_rows = jnp.minimum(starts[:, None] + frame_pos[None, :], own_rows - 1).reshape(-1)
    send_valid = (frame_pos[None, :] < lengths[:, None]).reshape(-1, 1)
    projected = jnp.dot(subsampled, proj_weight, preferred_element_type=jnp.float32).astype(
        jnp.bfloat16
    )
    outgoing = jnp.where(
        send_valid, jnp.take(projected, source_rows, axis=0), jnp.zeros((), jnp.bfloat16)
    )
    arrived = lax.all_to_all(
        outgoing.reshape(shards, MOST, part_width), "seq", split_axis=0, concat_axis=0, tiled=True
    )
    hidden_part = arrived.reshape(shards * MOST, part_width)
    hidden_full = lax.all_gather(hidden_part, "tp", axis=1, tiled=True)
    incoming = clip_dest == seq_index
    in_lengths = jnp.sum(jnp.where(incoming, clip_frames, 0), axis=1)
    valid = (frame_pos[None, :] < in_lengths[:, None]).reshape(-1, 1)
    mask = valid.astype(jnp.float32)
    hidden32 = hidden_full.astype(jnp.float32)
    centred = hidden32 - jnp.mean(hidden32, axis=1, keepdims=True)
    sigma = jnp.sqrt(jnp.mean(centred * centred, axis=1, keepdims=True) + 1e-05)
    normed = centred / sigma
    normed16 = normed.astype(jnp.bfloat16)
    value_pre = jnp.dot(normed16, value_weight, preferred_element_type=jnp.float32)
    gate_pre = jnp.dot(normed16, gate_weight, preferred_element_type=jnp.float32)
    gate_sig = jax.nn.sigmoid(gate_pre)
    glu = value_pre * gate_sig * mask
    conv = depthwise(glu.reshape(shards, MOST, part_width), conv_kernel).reshape(-1, part_width)
    conv_total, square_total = lax.psum(
        (jnp.sum(conv * mask, axis=0), jnp.sum(conv * conv * mask, axis=0)), "seq"
    )
    conv_mean = conv_total / count
    conv_var = square_total / count - conv_mean * conv_mean
    bn_scale = jnp.sqrt(conv_var + 1e-05)
    bn_hat = (conv - conv_mean) / bn_scale
    batch_normed = bn_gain * bn_hat + bn_shift
    bn_sig = jax.nn.sigmoid(batch_normed)
    swish = (batch_normed * bn_sig).astype(jnp.bfloat16)
    mixed = lax.psum_scatter(
        contract_cols(swish, down_weight), "tp", scatter_dimension=1, tiled=True
    )
    block_out = ((hidden_part.astype(jnp.float32) + mixed) * mask).astype(jnp.bfloat16)
    grad_out = jnp.where(valid, out_grad, jnp.zeros((), jnp.bfloat16))
    grad_full = lax.all_gather(grad_out, "tp", axis=1, tiled=True)
    down_local = contract_rows(grad_full, swish)
    grad_swish = jnp.dot(grad_full, down_weight, preferred_element_type=jnp.float32)
    grad_bn = grad_swish * bn_sig * (1.0 + batch_normed * (1.0 - bn_sig)) * mask
    bn_shift_grad, bn_gain_grad = lax.psum(
        (jnp.sum(grad_bn, axis=0), jnp.sum(grad_bn * bn_hat, axis=0)), "seq"
    )
    grad_conv = (
        bn_gain / bn_scale * (grad_bn - (bn_shift_grad + bn_hat * bn_gain_grad) / count) * mask
    )
    grad_glu = (
        depthwise_back(grad_conv.reshape(shards, MOST, part_width), conv_kernel).reshape(
            -1, part_width
        )
        * mask
    )
    grad_value = (grad_glu * gate_sig).astype(jnp.bfloat16)
    grad_gate = (grad_glu * value_pre * gate_sig * (1.0 - gate_sig)).astype(jnp.bfloat16)
    value_local = contract_rows(normed16, grad_value)
    gate_local = contract_rows(normed16, grad_gate)
    normed_terms = contract_cols(grad_value, value_weight) + contract_cols(grad_gate, gate_weight)
    grad_normed = lax.psum(normed_terms, "tp")
    grad_hidden = (
        grad_normed
        - jnp.mean(grad_normed, axis=1, keepdims=True)
        - normed * jnp.mean(grad_normed * normed, axis=1, keepdims=True)
    ) / sigma
    grad_hidden = lax.dynamic_slice_in_dim(grad_hidden, tp_index * part_width, part_width, 1)
    grad_packed = ((grad_out.astype(jnp.float32) + grad_hidden) * mask).astype(jnp.bfloat16)
    returned = lax.all_to_all(
        grad_packed.reshape(shards, MOST, part_width),
        "seq",
        split_axis=0,
        concat_axis=0,
        tiled=True,
    )
    row_ids = jnp.arange(own_rows, dtype=jnp.int32)
    clip_ends = jnp.cumsum(clip_lens)
    clip_of_row = jnp.sum((clip_ends[None, :] <= row_ids[:, None]).astype(jnp.int32), axis=1)
    row_match = clip_of_row[:, None] == shard_ids[None, :]
    row_start = jnp.sum(jnp.where(row_match, offsets[None, :], 0), axis=1)
    row_target = jnp.sum(jnp.where(row_match, clip_targets[None, :], 0), axis=1)
    positions = row_target * MOST + row_ids - row_start
    grad_proj = jnp.take(returned.reshape(shards * MOST, part_width), positions, axis=0)
    proj_local = contract_rows(subsampled, grad_proj)
    proj_grad, value_grad, gate_grad, down_grad = (
        lax.psum_scatter(proj_local, "seq", scatter_dimension=0, tiled=True),
        lax.psum_scatter(value_local, "seq", scatter_dimension=0, tiled=True),
        lax.psum_scatter(gate_local, "seq", scatter_dimension=0, tiled=True),
        lax.psum_scatter(down_local, "seq", scatter_dimension=0, tiled=True),
    )
    return (block_out, proj_grad, value_grad, gate_grad, down_grad, bn_gain_grad, bn_shift_grad)


def solution(mesh):
    placed = (
        P("seq", None),
        P(None, "tp"),
        P(None, "tp"),
        P(None, "tp"),
        P(None, "tp"),
        P("tp"),
        P("tp"),
        P(None, "tp"),
        P(),
        P(),
        P("seq", "tp"),
    )
    return jax.shard_map(
        body,
        mesh=mesh,
        in_specs=placed,
        out_specs=(
            P("seq", "tp"),
            P("seq", "tp"),
            P("seq", "tp"),
            P("seq", "tp"),
            P("seq", "tp"),
            P("tp"),
            P("tp"),
        ),
        check_vma=False,
    )
```

profile of v0, /device:TPU:0, one launch (start us, length us, event | category | flops | bytes accessed | tf_op | source)
XLA Modules:
  0.0 502.0 jit_solution(10994392400143319582)
XLA Ops:
  7.2 0.8 fusion.52
  8.1 0.2 reduce-window.4
  8.2 0.7 fusion.50
  9.0 0.1 select_reduce_fusion.4
  9.5 2.3 convolution_convert_fusion
  11.8 2.0 gather_fusion
  13.8 0.2 select_select_fusion
  14.0 16.1 %all_to_all.10 = bf16[8,64,256]{2,1,0:T(8,128)(2,1)} all-to-all(bf16[8,64,256]{2,1,0:T(8,128)(2,1)S(1)} %select_select_fusion), channel_id=1, replica_groups=mesh['seq'=8,'tp'=4] {'seq'}, dimensions={0} | all-to-all | bytes 524288 | tf_op jit(solution)/shard_map/all_to_all | solution.py:77
  30.2 0.1 select_reduce_fusion.2
  30.4 0.1 lt.106
  30.5 0.8 broadcast_select_fusion
  31.4 14.7 %all-gather.3.cloned.1.call-done = bf16[512,1024]{1,0:T(8,128)(2,1)} async-done(((bf16[512,256]{1,0:T(8,128)(2,1)}), bf16[512,1024]{1,0:T(8,128)(2,1)}) %all-gather.3.cloned.1.call-update) | async-done | bytes 1048592 | tf_op jit(solution)/shard_map/all_gather | solution.py:81
  46.1 1.5 convert_reduce_fusion
  47.6 1.6 fusion.2
  49.3 1.7 fusion.61
  51.0 0.5 fusion.6
  51.5 0.8 copy-done.6
  52.2 1.2 multiply_multiply_fusion.1
  53.5 1.5 multiply_reduce_fusion.3
  55.0 21.3 %all-reduce.3 = (f32[256]{0:T(256)S(1)}, f32[256]{0:T(256)S(1)}) all-reduce(f32[256]{0:T(256)S(1)} %get-tuple-element.31, f32[256]{0:T(256)S(1)} %get-tuple-element.30), channel_id=1, replica_groups=mesh['seq'=8,'tp'=4] {'seq'}, use_global_device_ids=true, to_apply=%region_9.10 | all-reduce | flops 512 | bytes 4096 | tf_op jit(solution)/shard_map/psum | solution.py:96
  76.3 1.9 fusion.44
  78.2 2.8 fusion.58
  81.0 17.1 %all-reduce.2 = (f32[256]{0:T(256)S(1)}, f32[256]{0:T(256)S(1)}) all-reduce(f32[256]{0:T(256)S(1)} %get-tuple-element.33, f32[256]{0:T(256)S(1)} %get-tuple-element.32), channel_id=1, replica_groups=mesh['seq'=8,'tp'=4] {'seq'}, use_global_device_ids=true, to_apply=%region_17.18 | all-reduce | flops 512 | bytes 4096 | tf_op jit(solution)/shard_map/psum | solution.py:115
  98.2 1.5 multiply_multiply_fusion
  99.7 0.5 fusion.32
  100.3 0.2 multiply_convert_fusion
  100.5 0.7 copy-done.5
  101.2 0.5 fusion.64
  101.7 1.8 convolution_add_fusion
  103.6 3.0 fusion.56
  106.7 0.1 select_reduce_fusion.1
  106.8 46.0 %all-reduce.6.cloned.1.call-done = f32[512,1024]{1,0:T(8,128)} async-done(((f32[512,1024]{1,0:T(8,128)}), f32[512,1024]{1,0:T(8,128)}) %all-reduce.6.cloned.1.call-update) | async-done | bytes 2097168 | tf_op jit(solution)/shard_map/psum | solution.py:132
  152.8 2.6 fusion.57
  155.5 31.4 %reduce-scatter.6.cloned.1.call-done = f32[512,256]{1,0:T(8,128)} async-done(((f32[512,1024]{1,0:T(8,128)}), f32[512,256]{1,0:T(8,128)}) %reduce-scatter.6.cloned.1.call-update) | async-done | bytes 524304 | tf_op jit(solution)/shard_map/reduce_scatter | solution.py:106
  186.9 2.6 fusion.45
  189.5 5.5 %all-to-all-start.1 = ((bf16[8,64,256]{2,1,0:T(8,128)(2,1)}), bf16[8,64,256]{2,1,0:T(8,128)(2,1)S(1)}, u32[]{:S(2)}, u32[]{:S(2)}) async-start(bf16[8,64,256]{2,1,0:T(8,128)(2,1)} %bitcast.70), calls=%async_computation.2 | async-start | bytes 524288 | tf_op jit(solution)/shard_map/all_to_all | solution.py:140
  195.1 8.8 %all-to-all-done.1 = bf16[8,64,256]{2,1,0:T(8,128)(2,1)S(1)} async-done(((bf16[8,64,256]{2,1,0:T(8,128)(2,1)}), bf16[8,64,256]{2,1,0:T(8,128)(2,1)S(1)}, u32[]{:S(2)}, u32[]{:S(2)}) %all-to-all-start.1) | async-done | bytes 262176 | tf_op jit(solution)/shard_map/all_to_all | solution.py:140
  203.9 1.2 gather_fusion.1
  205.1 2.7 convolution_bitcast_fusion
  207.9 0.6 copy-done.21
  208.5 2.9 fusion.55
  211.5 2.4 fusion.65
  214.0 1.5 fusion.66
  215.5 79.0 %reduce-scatter.8.cloned.1.call-done = f32[512,256]{0,1:T(8,128)} async-done(((f32[4096,256]{0,1:T(8,128)}), f32[512,256]{0,1:T(8,128)}) %reduce-scatter.8.cloned.1.call-update) | async-done | bytes 524304 | tf_op jit(solution)/shard_map/reduce_scatter | solution.py:157
  294.6 2.0 copy.20
  296.6 65.3 %reduce-scatter.14.cloned.1.call-done = f32[128,256]{1,0:T(8,128)} async-done(((f32[1024,256]{1,0:T(8,128)}), f32[128,256]{1,0:T(8,128)}) %reduce-scatter.14.cloned.1.call-update) | async-done | bytes 131088 | tf_op jit(solution)/shard_map/reduce_scatter | solution.py:160
  361.9 66.5 %reduce-scatter.10.cloned.1.call-done = f32[128,256]{1,0:T(8,128)} async-done(((f32[1024,256]{1,0:T(8,128)}), f32[128,256]{1,0:T(8,128)}) %reduce-scatter.10.cloned.1.call-update) | async-done | bytes 131088 | tf_op jit(solution)/shard_map/reduce_scatter | solution.py:158
  428.4 66.8 %reduce-scatter.12.cloned.1.call-done = f32[128,256]{1,0:T(8,128)} async-done(((f32[1024,256]{1,0:T(8,128)}), f32[128,256]{1,0:T(8,128)}) %reduce-scatter.12.cloned.1.call-update) | async-done | bytes 131088 | tf_op jit(solution)/shard_map/reduce_scatter | solution.py:159
  (77 shorter events, 1.1 us)
Async XLA Ops:
  7.2 2.3 copy-start
  7.2 38.9 %all-gather.3.cloned.1.call-start = ((), (), s32[]{:S(2)}) async-start(), calls=%async_computation.7 | async-start | bytes 1310720 | tf_op jit(solution)/shard_map/all_gather | solution.py:81
  11.8 18.4 %copy-start.15 = (s32[8,8]{1,0:T(8,128)S(1)}, s32[8,8]{1,0:T(8,128)}, u32[]{:S(2)}) copy-start(s32[8,8]{1,0:T(8,128)} %param.19) | copy-start | bytes 772
  11.8 18.4 %copy-start.16 = (s32[8,8]{1,0:T(8,128)S(1)}, s32[8,8]{1,0:T(8,128)}, u32[]{:S(2)}) copy-start(s32[8,8]{1,0:T(8,128)} %param.20) | copy-start | bytes 772
  11.8 18.7 %copy-start.11 = (bf16[512,256]{1,0:T(8,128)(2,1)S(1)}, bf16[512,256]{1,0:T(8,128)(2,1)}, u32[]{:S(2)}) copy-start(bf16[512,256]{1,0:T(8,128)(2,1)} %param.21) | copy-start | bytes 786436
  11.8 19.6 %copy-start.14 = (f32[9,256]{1,0:T(8,128)S(1)}, f32[9,256]{1,0:T(8,128)}, u32[]{:S(2)}) copy-start(f32[9,256]{1,0:T(8,128)} %param.15) | copy-start | bytes 27652
  30.1 48.1 %all-gather.5.cloned.1.call-start = ((), (), s32[]{:S(2)}) async-start(), calls=%async_computation.9 | async-start | bytes 1310720 | tf_op jit(solution)/shard_map/all_gather | solution.py:111
  31.3 121.5 %all-reduce.6.cloned.1.call-start = ((), (), s32[]{:S(2)}) async-start(), calls=%async_computation.10 | async-start | bytes 4194304 | tf_op jit(solution)/shard_map/psum | solution.py:132
  46.1 3.2 copy-start.1
  49.3 1.7 copy-start.12
  51.0 1.3 copy-start.9
  51.4 0.8 copy-start.6
  52.2 24.1 %copy-start.17 = (f32[256]{0:T(256)S(1)}, f32[256]{0:T(256)}, u32[]{:S(2)}) copy-start(f32[256]{0:T(256)} %param.16) | copy-start | bytes 3076
  52.2 26.0 %copy-start.20 = (f32[256]{0:T(256)S(1)}, f32[256]{0:T(256)}, u32[]{:S(2)}) copy-start(f32[256]{0:T(256)} %param.17) | copy-start | bytes 3076
  98.2 2.3 copy-start.18
  98.2 2.3 copy-start.19
  98.2 2.1 copy-start.7
  98.2 2.1 copy-start.8
  98.2 3.0 copy-start.10
  100.2 1.4 copy-start.13
  100.5 0.7 copy-start.5
  100.5 1.2 copy-start.2
  103.5 83.4 %reduce-scatter.6.cloned.1.call-start = ((), (), s32[]{:S(2)}) async-start(), calls=%async_computation.8 | async-start | bytes 2621440 | tf_op jit(solution)/shard_map/reduce_scatter | solution.py:106
  152.8 34.1 %copy-start.4 = (bf16[8,64,256]{2,1,0:T(8,128)(2,1)S(1)}, bf16[8,64,256]{2,1,0:T(8,128)(2,1)}, u32[]{:S(2)}) copy-start(bf16[8,64,256]{2,1,0:T(8,128)(2,1)} %all_to_all.10) | copy-start | bytes 786436
  189.5 14.4 %all-to-all-start.1 = ((bf16[8,64,256]{2,1,0:T(8,128)(2,1)}), bf16[8,64,256]{2,1,0:T(8,128)(2,1)S(1)}, u32[]{:S(2)}, u32[]{:S(2)}) async-start(bf16[8,64,256]{2,1,0:T(8,128)(2,1)} %bitcast.70), calls=%async_computation.2 | async-start | bytes 524288 | tf_op jit(solution)/shard_map/all_to_all | solution.py:140
  195.0 99.5 %reduce-scatter.8.cloned.1.call-start = ((), (), s32[]{:S(2)}) async-start(), calls=%async_computation.11 | async-start | bytes 4718592 | tf_op jit(solution)/shard_map/reduce_scatter | solution.py:157
  207.8 0.7 copy-start.21
  207.9 154.0 %reduce-scatter.14.cloned.1.call-start = ((), (), s32[]{:S(2)}) async-start(), calls=%async_computation.14 | async-start | bytes 1179648 | tf_op jit(solution)/shard_map/reduce_scatter | solution.py:160
  211.4 2.6 copy-start.3
  211.5 216.9 %reduce-scatter.10.cloned.1.call-start = ((), (), s32[]{:S(2)}) async-start(), calls=%async_computation.12 | async-start | bytes 1179648 | tf_op jit(solution)/shard_map/reduce_scatter | solution.py:158
  214.0 281.2 %reduce-scatter.12.cloned.1.call-start = ((), (), s32[]{:S(2)}) async-start(), calls=%async_computation.13 | async-start | bytes 1179648 | tf_op jit(solution)/shard_map/reduce_scatter | solution.py:159
Sparse Core Ops, SparseCore 0:
  30.2 15.8 all-gather.2
  48.2 16.8 all-gather.4
  103.6 49.1 all-reduce.5
  155.4 31.4 reduce-scatter.5
  208.0 86.5 reduce-scatter.7
  298.8 63.0 reduce-scatter.13
  365.9 62.4 reduce-scatter.9
  432.7 62.3 reduce-scatter.11
where the time goes:
time: 503 us; the launch traced here: 502 us
  waiting for transfers between devices  379 us (75%)
  blocking collectives  54.6 us (11%)
  matrix products  21.7 us (4%)
  other arithmetic  18.4 us (4%)
  between operations  14.5 us (3%)
  local copies, waits for them, and re-layouts  8.33 us (2%)
  starting transfers between devices  5.84 us (1%)
    reduce_scatter x1, waiting for transfers between devices, body(): lax.psum_scatter(proj_local, 'seq', scatter_dimension=0, tiled=True)  79 us
    reduce_scatter x1, waiting for transfers between devices, body(): lax.psum_scatter(gate_local, 'seq', scatter_dimension=0, tiled=True)  66.8 us
    reduce_scatter x1, waiting for transfers between devices, body(): lax.psum_scatter(value_local, 'seq', scatter_dimension=0, tiled=True)  66.5 us
    reduce_scatter x1, waiting for transfers between devices, body(): lax.psum_scatter(down_local, 'seq', scatter_dimension=0, tiled=True)  65.3 us
    psum x1, waiting for transfers between devices, body(): grad_normed = lax.psum(normed_terms, 'tp')  46 us
    reduce_scatter x1, waiting for transfers between devices, body(): lax.psum_scatter(contract_cols(swish, down_weight), 'tp', scatter_dimensi...  31.4 us
    psum x1, blocking collectives, body(): lax.psum((jnp.sum(conv * mask, axis=0), jnp.sum(conv * conv * mask, axis=...  21.3 us
    psum x1, blocking collectives, body(): lax.psum((jnp.sum(grad_bn, axis=0), jnp.sum(grad_bn * bn_hat, axis=0)), '...  17.1 us
  transfers between devices with their start and end apart: 9, of which 8 were waited for; matrix products, arithmetic and copies ran while one was open for 5% of the time, Pallas kernels for 0%

commit v1 on v0

--- a/solution.py
+++ b/solution.py
@@ -60,8 +60,9 @@
     count = float(own_rows * shards)
     clip_lens = lax.dynamic_slice_in_dim(clip_frames, seq_index, 1, 0)[0]
     clip_targets = lax.dynamic_slice_in_dim(clip_dest, seq_index, 1, 0)[0]
-    offsets = jnp.cumsum(clip_lens) - clip_lens
     shard_ids = jnp.arange(shards, dtype=jnp.int32)
+    earlier = shard_ids[None, :] < shard_ids[:, None]
+    offsets = jnp.sum(jnp.where(earlier, clip_lens[None, :], 0), axis=1)
     match = clip_targets[None, :] == shard_ids[:, None]
     starts = jnp.sum(jnp.where(match, offsets[None, :], 0), axis=1)
     lengths = jnp.sum(jnp.where(match, clip_lens[None, :], 0), axis=1)
@@ -145,7 +146,7 @@
         tiled=True,
     )
     row_ids = jnp.arange(own_rows, dtype=jnp.int32)
-    clip_ends = jnp.cumsum(clip_lens)
+    clip_ends = offsets + clip_lens
     clip_of_row = jnp.sum((clip_ends[None, :] <= row_ids[:, None]).astype(jnp.int32), axis=1)
     row_match = clip_of_row[:, None] == shard_ids[None, :]
     row_start = jnp.sum(jnp.where(row_match, offsets[None, :], 0), axis=1)

time: 503 us -> 503 us (level)
  no operation moved by 1% of the time
where the time goes in v1:
time: 503 us; the launch traced here: 502 us
  waiting for transfers between devices  379 us (75%)
  blocking collectives  54.6 us (11%)
  matrix products  21.7 us (4%)
  other arithmetic  18.4 us (4%)
  between operations  14.5 us (3%)
  local copies, waits for them, and re-layouts  8.33 us (2%)
  starting transfers between devices  5.84 us (1%)
    reduce_scatter x1, waiting for transfers between devices, body(): lax.psum_scatter(proj_local, 'seq', scatter_dimension=0, tiled=True)  79 us
    reduce_scatter x1, waiting for transfers between devices, body(): lax.psum_scatter(gate_local, 'seq', scatter_dimension=0, tiled=True)  66.9 us
    reduce_scatter x1, waiting for transfers between devices, body(): lax.psum_scatter(value_local, 'seq', scatter_dimension=0, tiled=True)  66.5 us
    reduce_scatter x1, waiting for transfers between devices, body(): lax.psum_scatter(down_local, 'seq', scatter_dimension=0, tiled=True)  65.3 us
    psum x1, waiting for transfers between devices, body(): grad_normed = lax.psum(normed_terms, 'tp')  46 us
    reduce_scatter x1, waiting for transfers between devices, body(): lax.psum_scatter(contract_cols(swish, down_weight), 'tp', scatter_dimensi...  31.4 us
    psum x1, blocking collectives, body(): lax.psum((jnp.sum(conv * mask, axis=0), jnp.sum(conv * conv * mask, axis=...  21.3 us
    psum x1, blocking collectives, body(): lax.psum((jnp.sum(grad_bn, axis=0), jnp.sum(grad_bn * bn_hat, axis=0)), '...  17.1 us
  transfers between devices with their start and end apart: 9, of which 8 were waited for; matrix products, arithmetic and copies ran while one was open for 5% of the time, Pallas kernels for 0%

profile of v1, /device:TPU:0, one launch (start us, length us, event | category | flops | bytes accessed | tf_op | source)
XLA Modules:
  0.0 502.0 jit_solution(3693335612410852194)
XLA Ops:
  7.2 0.8 fusion.51
  8.1 0.1 select_reduce_fusion.4
  8.2 0.7 fusion.49
  8.9 0.1 select_reduce_fusion.5
  9.4 2.3 convolution_convert_fusion
  11.7 2.0 gather_fusion
  13.7 0.2 select_select_fusion
  13.9 16.1 %all_to_all.10 = bf16[8,64,256]{2,1,0:T(8,128)(2,1)} all-to-all(bf16[8,64,256]{2,1,0:T(8,128)(2,1)S(1)} %select_select_fusion), channel_id=1, replica_groups=mesh['seq'=8,'tp'=4] {'seq'}, dimensions={0} | all-to-all | bytes 524288 | tf_op jit(solution)/shard_map/all_to_all | solution.py:78
  30.1 0.1 select_reduce_fusion.2
  30.3 0.1 lt.119
  30.4 0.8 broadcast_select_fusion
  31.4 14.7 %all-gather.3.cloned.1.call-done = bf16[512,1024]{1,0:T(8,128)(2,1)} async-done(((bf16[512,256]{1,0:T(8,128)(2,1)}), bf16[512,1024]{1,0:T(8,128)(2,1)}) %all-gather.3.cloned.1.call-update) | async-done | bytes 1048592 | tf_op jit(solution)/shard_map/all_gather | solution.py:82
  46.0 1.5 convert_reduce_fusion
  47.6 1.6 fusion.2
  49.2 1.7 fusion.60
  50.9 0.5 fusion.6
  51.4 0.8 copy-done.6
  52.2 1.2 multiply_multiply_fusion.1
  53.4 1.5 multiply_reduce_fusion.3
  54.9 21.3 %all-reduce.3 = (f32[256]{0:T(256)S(1)}, f32[256]{0:T(256)S(1)}) all-reduce(f32[256]{0:T(256)S(1)} %get-tuple-element.31, f32[256]{0:T(256)S(1)} %get-tuple-element.30), channel_id=1, replica_groups=mesh['seq'=8,'tp'=4] {'seq'}, use_global_device_ids=true, to_apply=%region_9.10 | all-reduce | flops 512 | bytes 4096 | tf_op jit(solution)/shard_map/psum | solution.py:97
  76.3 1.9 fusion.44
  78.1 2.8 fusion.57
  81.0 17.1 %all-reduce.2 = (f32[256]{0:T(256)S(1)}, f32[256]{0:T(256)S(1)}) all-reduce(f32[256]{0:T(256)S(1)} %get-tuple-element.33, f32[256]{0:T(256)S(1)} %get-tuple-element.32), channel_id=1, replica_groups=mesh['seq'=8,'tp'=4] {'seq'}, use_global_device_ids=true, to_apply=%region_17.18 | all-reduce | flops 512 | bytes 4096 | tf_op jit(solution)/shard_map/psum | solution.py:116
  98.1 1.5 multiply_multiply_fusion
  99.6 0.5 fusion.32
  100.2 0.2 multiply_convert_fusion
  100.4 0.7 copy-done.5
  101.1 0.5 fusion.63
  101.6 1.8 convolution_add_fusion
  103.5 3.0 fusion.55
  106.6 0.1 select_reduce_fusion.1
  106.7 46.0 %all-reduce.6.cloned.1.call-done = f32[512,1024]{1,0:T(8,128)} async-done(((f32[512,1024]{1,0:T(8,128)}), f32[512,1024]{1,0:T(8,128)}) %all-reduce.6.cloned.1.call-update) | async-done | bytes 2097168 | tf_op jit(solution)/shard_map/psum | solution.py:133
  152.8 2.6 fusion.56
  155.4 31.4 %reduce-scatter.6.cloned.1.call-done = f32[512,256]{1,0:T(8,128)} async-done(((f32[512,1024]{1,0:T(8,128)}), f32[512,256]{1,0:T(8,128)}) %reduce-scatter.6.cloned.1.call-update) | async-done | bytes 524304 | tf_op jit(solution)/shard_map/reduce_scatter | solution.py:107
  186.8 2.6 fusion.45
  189.5 5.5 %all-to-all-start.1 = ((bf16[8,64,256]{2,1,0:T(8,128)(2,1)}), bf16[8,64,256]{2,1,0:T(8,128)(2,1)S(1)}, u32[]{:S(2)}, u32[]{:S(2)}) async-start(bf16[8,64,256]{2,1,0:T(8,128)(2,1)} %bitcast.67), calls=%async_computation.2 | async-start | bytes 524288 | tf_op jit(solution)/shard_map/all_to_all | solution.py:141
  195.1 8.8 %all-to-all-done.1 = bf16[8,64,256]{2,1,0:T(8,128)(2,1)S(1)} async-done(((bf16[8,64,256]{2,1,0:T(8,128)(2,1)}), bf16[8,64,256]{2,1,0:T(8,128)(2,1)S(1)}, u32[]{:S(2)}, u32[]{:S(2)}) %all-to-all-start.1) | async-done | bytes 262176 | tf_op jit(solution)/shard_map/all_to_all | solution.py:141
  203.9 1.2 gather_fusion.1
  205.0 2.7 convolution_bitcast_fusion
  207.9 0.6 copy-done.21
  208.5 2.9 fusion.54
  211.4 2.4 fusion.64
  214.0 1.5 fusion.65
  215.5 79.0 %reduce-scatter.8.cloned.1.call-done = f32[512,256]{0,1:T(8,128)} async-done(((f32[4096,256]{0,1:T(8,128)}), f32[512,256]{0,1:T(8,128)}) %reduce-scatter.8.cloned.1.call-update) | async-done | bytes 524304 | tf_op jit(solution)/shard_map/reduce_scatter | solution.py:158
  294.5 2.0 copy.20
  296.5 65.3 %reduce-scatter.14.cloned.1.call-done = f32[128,256]{1,0:T(8,128)} async-done(((f32[1024,256]{1,0:T(8,128)}), f32[128,256]{1,0:T(8,128)}) %reduce-scatter.14.cloned.1.call-update) | async-done | bytes 131088 | tf_op jit(solution)/shard_map/reduce_scatter | solution.py:161
  361.9 66.5 %reduce-scatter.10.cloned.1.call-done = f32[128,256]{1,0:T(8,128)} async-done(((f32[1024,256]{1,0:T(8,128)}), f32[128,256]{1,0:T(8,128)}) %reduce-scatter.10.cloned.1.call-update) | async-done | bytes 131088 | tf_op jit(solution)/shard_map/reduce_scatter | solution.py:159
  428.3 66.9 %reduce-scatter.12.cloned.1.call-done = f32[128,256]{1,0:T(8,128)} async-done(((f32[1024,256]{1,0:T(8,128)}), f32[128,256]{1,0:T(8,128)}) %reduce-scatter.12.cloned.1.call-update) | async-done | bytes 131088 | tf_op jit(solution)/shard_map/reduce_scatter | solution.py:160
  (77 shorter events, 1.1 us)
Async XLA Ops:
  7.2 2.2 copy-start
  7.2 38.9 %all-gather.3.cloned.1.call-start = ((), (), s32[]{:S(2)}) async-start(), calls=%async_computation.7 | async-start | bytes 1310720 | tf_op jit(solution)/shard_map/all_gather | solution.py:82
  11.7 18.4 %copy-start.15 = (s32[8,8]{1,0:T(8,128)S(1)}, s32[8,8]{1,0:T(8,128)}, u32[]{:S(2)}) copy-start(s32[8,8]{1,0:T(8,128)} %param.19) | copy-start | bytes 772
  11.7 18.4 %copy-start.16 = (s32[8,8]{1,0:T(8,128)S(1)}, s32[8,8]{1,0:T(8,128)}, u32[]{:S(2)}) copy-start(s32[8,8]{1,0:T(8,128)} %param.20) | copy-start | bytes 772
  11.7 18.7 %copy-start.11 = (bf16[512,256]{1,0:T(8,128)(2,1)S(1)}, bf16[512,256]{1,0:T(8,128)(2,1)}, u32[]{:S(2)}) copy-start(bf16[512,256]{1,0:T(8,128)(2,1)} %param.21) | copy-start | bytes 786436
  11.7 19.6 %copy-start.14 = (f32[9,256]{1,0:T(8,128)S(1)}, f32[9,256]{1,0:T(8,128)}, u32[]{:S(2)}) copy-start(f32[9,256]{1,0:T(8,128)} %param.15) | copy-start | bytes 27652
  30.0 48.1 %all-gather.5.cloned.1.call-start = ((), (), s32[]{:S(2)}) async-start(), calls=%async_computation.9 | async-start | bytes 1310720 | tf_op jit(solution)/shard_map/all_gather | solution.py:112
  31.3 121.5 %all-reduce.6.cloned.1.call-start = ((), (), s32[]{:S(2)}) async-start(), calls=%async_computation.10 | async-start | bytes 4194304 | tf_op jit(solution)/shard_map/psum | solution.py:133
  46.0 3.2 copy-start.1
  49.2 1.7 copy-start.12
  50.9 1.3 copy-start.9
  51.4 0.8 copy-start.6
  52.2 24.1 %copy-start.17 = (f32[256]{0:T(256)S(1)}, f32[256]{0:T(256)}, u32[]{:S(2)}) copy-start(f32[256]{0:T(256)} %param.16) | copy-start | bytes 3076
  52.2 26.0 %copy-start.20 = (f32[256]{0:T(256)S(1)}, f32[256]{0:T(256)}, u32[]{:S(2)}) copy-start(f32[256]{0:T(256)} %param.17) | copy-start | bytes 3076
  98.1 2.3 copy-start.18
  98.1 2.3 copy-start.19
  98.1 2.1 copy-start.7
  98.1 2.1 copy-start.8
  98.1 3.0 copy-start.10
  100.2 1.4 copy-start.13
  100.4 0.7 copy-start.5
  100.4 1.2 copy-start.2
  103.5 83.4 %reduce-scatter.6.cloned.1.call-start = ((), (), s32[]{:S(2)}) async-start(), calls=%async_computation.8 | async-start | bytes 2621440 | tf_op jit(solution)/shard_map/reduce_scatter | solution.py:107
  152.8 34.1 %copy-start.4 = (bf16[8,64,256]{2,1,0:T(8,128)(2,1)S(1)}, bf16[8,64,256]{2,1,0:T(8,128)(2,1)}, u32[]{:S(2)}) copy-start(bf16[8,64,256]{2,1,0:T(8,128)(2,1)} %all_to_all.10) | copy-start | bytes 786436
  189.5 14.4 %all-to-all-start.1 = ((bf16[8,64,256]{2,1,0:T(8,128)(2,1)}), bf16[8,64,256]{2,1,0:T(8,128)(2,1)S(1)}, u32[]{:S(2)}, u32[]{:S(2)}) async-start(bf16[8,64,256]{2,1,0:T(8,128)(2,1)} %bitcast.67), calls=%async_computation.2 | async-start | bytes 524288 | tf_op jit(solution)/shard_map/all_to_all | solution.py:141
  195.0 99.5 %reduce-scatter.8.cloned.1.call-start = ((), (), s32[]{:S(2)}) async-start(), calls=%async_computation.11 | async-start | bytes 4718592 | tf_op jit(solution)/shard_map/reduce_scatter | solution.py:158
  207.8 0.7 copy-start.21
  207.8 154.0 %reduce-scatter.14.cloned.1.call-start = ((), (), s32[]{:S(2)}) async-start(), calls=%async_computation.14 | async-start | bytes 1179648 | tf_op jit(solution)/shard_map/reduce_scatter | solution.py:161
  211.4 2.6 copy-start.3
  211.4 216.9 %reduce-scatter.10.cloned.1.call-start = ((), (), s32[]{:S(2)}) async-start(), calls=%async_computation.12 | async-start | bytes 1179648 | tf_op jit(solution)/shard_map/reduce_scatter | solution.py:159
  213.9 281.3 %reduce-scatter.12.cloned.1.call-start = ((), (), s32[]{:S(2)}) async-start(), calls=%async_computation.13 | async-start | bytes 1179648 | tf_op jit(solution)/shard_map/reduce_scatter | solution.py:160
Sparse Core Ops, SparseCore 0:
  30.2 15.8 all-gather.2
  48.2 16.8 all-gather.4
  103.6 49.1 all-reduce.5
  155.3 31.4 reduce-scatter.5
  207.9 86.5 reduce-scatter.7
  298.7 63.0 reduce-scatter.13
  365.8 62.4 reduce-scatter.9
  432.7 62.4 reduce-scatter.11

commit v2 on v1

--- a/solution.py
+++ b/solution.py
@@ -1,9 +1,105 @@
+import functools
 import jax
 import jax.numpy as jnp
 from jax import lax
+from jax.experimental import pallas as pl
+from jax.experimental.pallas import tpu as pltpu
 from jax.sharding import PartitionSpec as P
 
 MOST = 64
+
+
+def source_of(kind, ref, index):
+    if kind == "rows":
+        return ref.at[index]
+    if kind == "split":
+        width = ref.shape[1] // lax.axis_size("tp")
+        return ref.at[:, pl.ds(pl.multiple_of(index * width, 128), width)]
+    return ref
+
+
+def target_of(kind, ref, index, width):
+    if kind == "columns":
+        return ref.at[:, pl.ds(pl.multiple_of(index * width, 128), width)]
+    return ref.at[index]
+
+
+def transfer_kernel(plan, *refs):
+    count = len(plan)
+    sources, targets = refs[:count], refs[count : 2 * count]
+    sends, recvs, local_sem = refs[2 * count : 3 * count], refs[3 * count : 4 * count], refs[4 * count]
+    barrier = pltpu.get_barrier_semaphore()
+    greeted = 0
+    for axis in sorted({axis for _, axis in plan}):
+        size = lax.axis_size(axis)
+        me = lax.axis_index(axis)
+        for step in range(1, size):
+            peer = lax.rem(me + step, size)
+            pl.semaphore_signal(
+                barrier, inc=1, device_id={axis: peer}, device_id_type=pl.DeviceIdType.MESH
+            )
+        greeted += size - 1
+    pl.semaphore_wait(barrier, greeted)
+    copies = []
+    for which, (kind, axis) in enumerate(plan):
+        size = lax.axis_size(axis)
+        me = lax.axis_index(axis)
+        source, target = sources[which], targets[which]
+        width = source.shape[-1]
+        for step in range(1, size):
+            peer = lax.rem(me + step, size)
+            copy = pltpu.make_async_remote_copy(
+                src_ref=source_of(kind, source, peer),
+                dst_ref=target_of(kind, target, me, width),
+                send_sem=sends[which].at[step],
+                recv_sem=recvs[which].at[step],
+                device_id={axis: peer},
+                device_id_type=pl.DeviceIdType.MESH,
+            )
+            copy.start()
+            copies.append(copy)
+        own = pltpu.make_async_copy(
+            source_of(kind, source, me), target_of(kind, target, me, width), local_sem.at[which]
+        )
+        own.start()
+        copies.append(own)
+    for copy in copies:
+        copy.wait()
+
+
+def transfer(number, *items):
+    plan = tuple((kind, axis) for kind, axis, _ in items)
+    arrays = [array for _, _, array in items]
+    outs = []
+    for kind, axis, array in items:
+        size = lax.axis_size(axis)
+        if kind == "rows":
+            shape = array.shape
+        elif kind == "split":
+            shape = (size, array.shape[0], array.shape[1] // size)
+        elif kind == "columns":
+            shape = (array.shape[0], array.shape[1] * size)
+        else:
+            shape = (size,) + array.shape
+        outs.append(jax.ShapeDtypeStruct(shape, array.dtype))
+    sems = [pltpu.SemaphoreType.DMA((lax.axis_size(axis),)) for _, axis in plan]
+    return pl.pallas_call(
+        functools.partial(transfer_kernel, plan),
+        out_shape=outs,
+        in_specs=[pl.BlockSpec(memory_space=pl.ANY)] * len(arrays),
+        out_specs=[pl.BlockSpec(memory_space=pl.ANY)] * len(arrays),
+        scratch_shapes=sems + sems + [pltpu.SemaphoreType.DMA((len(plan),))],
+        compiler_params=pltpu.CompilerParams(collective_id=number, has_side_effects=True),
+    )(*arrays)
+
+
+def summed(parts):
+    return jnp.sum(parts.astype(jnp.float32), axis=0)
+
+
+def stacked(first, second):
+    empty = jnp.zeros((6,) + first.shape, jnp.float32)
+    return jnp.concatenate([first[None], second[None], empty], axis=0)
 
 
 def depthwise(field, kernel):
@@ -75,15 +171,18 @@
     outgoing = jnp.where(
         send_valid, jnp.take(projected, source_rows, axis=0), jnp.zeros((), jnp.bfloat16)
     )
-    arrived = lax.all_to_all(
-        outgoing.reshape(shards, MOST, part_width), "seq", split_axis=0, concat_axis=0, tiled=True
-    )
-    hidden_part = arrived.reshape(shards * MOST, part_width)
-    hidden_full = lax.all_gather(hidden_part, "tp", axis=1, tiled=True)
     incoming = clip_dest == seq_index
     in_lengths = jnp.sum(jnp.where(incoming, clip_frames, 0), axis=1)
     valid = (frame_pos[None, :] < in_lengths[:, None]).reshape(-1, 1)
     mask = valid.astype(jnp.float32)
+    grad_out = jnp.where(valid, out_grad, jnp.zeros((), jnp.bfloat16))
+    arrived, grad_full = transfer(
+        1,
+        ("rows", "seq", outgoing.reshape(shards, MOST, part_width)),
+        ("columns", "tp", grad_out),
+    )
+    hidden_part = arrived.reshape(shards * MOST, part_width)
+    (hidden_full,) = transfer(2, ("columns", "tp", hidden_part))
     hidden32 = hidden_full.astype(jnp.float32)
     centred = hidden32 - jnp.mean(hidden32, axis=1, keepdims=True)
     sigma = jnp.sqrt(jnp.mean(centred * centred, axis=1, keepdims=True) + 1e-05)
@@ -94,9 +193,11 @@
     gate_sig = jax.nn.sigmoid(gate_pre)
     glu = value_pre * gate_sig * mask
     conv = depthwise(glu.reshape(shards, MOST, part_width), conv_kernel).reshape(-1, part_width)
-    conv_total, square_total = lax.psum(
-        (jnp.sum(conv * mask, axis=0), jnp.sum(conv * conv * mask, axis=0)), "seq"
-    )
+    (conv_parts,) = transfer(
+        3, ("whole", "seq", stacked(jnp.sum(conv * mask, axis=0), jnp.sum(conv * conv * mask, axis=0)))
+    )
+    conv_sums = summed(conv_parts)
+    conv_total, square_total = conv_sums[0], conv_sums[1]
     conv_mean = conv_total / count
     conv_var = square_total / count - conv_mean * conv_mean
     bn_scale = jnp.sqrt(conv_var + 1e-05)
@@ -104,18 +205,15 @@
     batch_normed = bn_gain * bn_hat + bn_shift
     bn_sig = jax.nn.sigmoid(batch_normed)
     swish = (batch_normed * bn_sig).astype(jnp.bfloat16)
-    mixed = lax.psum_scatter(
-        contract_cols(swish, down_weight), "tp", scatter_dimension=1, tiled=True
-    )
-    block_out = ((hidden_part.astype(jnp.float32) + mixed) * mask).astype(jnp.bfloat16)
-    grad_out = jnp.where(valid, out_grad, jnp.zeros((), jnp.bfloat16))
-    grad_full = lax.all_gather(grad_out, "tp", axis=1, tiled=True)
+    mixed_local = contract_cols(swish, down_weight).astype(jnp.bfloat16)
     down_local = contract_rows(grad_full, swish)
     grad_swish = jnp.dot(grad_full, down_weight, preferred_element_type=jnp.float32)
     grad_bn = grad_swish * bn_sig * (1.0 + batch_normed * (1.0 - bn_sig)) * mask
-    bn_shift_grad, bn_gain_grad = lax.psum(
-        (jnp.sum(grad_bn, axis=0), jnp.sum(grad_bn * bn_hat, axis=0)), "seq"
-    )
+    (bn_parts,) = transfer(
+        4, ("whole", "seq", stacked(jnp.sum(grad_bn, axis=0), jnp.sum(grad_bn * bn_hat, axis=0)))
+    )
+    bn_sums = summed(bn_parts)
+    bn_shift_grad, bn_gain_grad = bn_sums[0], bn_sums[1]
     grad_conv = (
         bn_gain / bn_scale * (grad_bn - (bn_shift_grad + bn_hat * bn_gain_grad) / count) * mask
     )
@@ -130,21 +228,34 @@
     value_local = contract_rows(normed16, grad_value)
     gate_local = contract_rows(normed16, grad_gate)
     normed_terms = contract_cols(grad_value, value_weight) + contract_cols(grad_gate, gate_weight)
-    grad_normed = lax.psum(normed_terms, "tp")
-    grad_hidden = (
-        grad_normed
-        - jnp.mean(grad_normed, axis=1, keepdims=True)
-        - normed * jnp.mean(grad_normed * normed, axis=1, keepdims=True)
-    ) / sigma
-    grad_hidden = lax.dynamic_slice_in_dim(grad_hidden, tp_index * part_width, part_width, 1)
+    row_sums = stacked(jnp.sum(normed_terms, axis=1), jnp.sum(normed_terms * normed, axis=1))
+    width_all = normed.shape[1]
+    weight_parts = jnp.concatenate(
+        [
+            part.astype(jnp.bfloat16).reshape(shards, width_all // shards, part_width)
+            for part in (value_local, gate_local, down_local)
+        ],
+        axis=1,
+    )
+    normed_parts, row_parts, weight_blocks = transfer(
+        5,
+        ("split", "tp", normed_terms.astype(jnp.bfloat16)),
+        ("whole", "tp", row_sums),
+        ("rows", "seq", weight_parts),
+    )
+    row_means = (summed(row_parts) / width_all).T
+    normed_own = lax.dynamic_slice_in_dim(normed, tp_index * part_width, part_width, 1)
+    grad_hidden = (summed(normed_parts) - row_means[:, 0:1] - normed_own * row_means[:, 1:2]) / sigma
     grad_packed = ((grad_out.astype(jnp.float32) + grad_hidden) * mask).astype(jnp.bfloat16)
-    returned = lax.all_to_all(
-        grad_packed.reshape(shards, MOST, part_width),
-        "seq",
-        split_axis=0,
-        concat_axis=0,
-        tiled=True,
-    )
+    returned, mixed_parts = transfer(
+        6,
+        ("rows", "seq", grad_packed.reshape(shards, MOST, part_width)),
+        ("split", "tp", mixed_local),
+    )
+    block_out = ((hidden_part.astype(jnp.float32) + summed(mixed_parts)) * mask).astype(
+        jnp.bfloat16
+    )
+    value_grad, gate_grad, down_grad = jnp.split(summed(weight_blocks), 3, axis=0)
     row_ids = jnp.arange(own_rows, dtype=jnp.int32)
     clip_ends = offsets + clip_lens
     clip_of_row = jnp.sum((clip_ends[None, :] <= row_ids[:, None]).astype(jnp.int32), axis=1)
@@ -154,12 +265,17 @@
     positions = row_target * MOST + row_ids - row_start
     grad_proj = jnp.take(returned.reshape(shards * MOST, part_width), positions, axis=0)
     proj_local = contract_rows(subsampled, grad_proj)
-    proj_grad, value_grad, gate_grad, down_grad = (
-        lax.psum_scatter(proj_local, "seq", scatter_dimension=0, tiled=True),
-        lax.psum_scatter(value_local, "seq", scatter_dimension=0, tiled=True),
-        lax.psum_scatter(gate_local, "seq", scatter_dimension=0, tiled=True),
-        lax.psum_scatter(down_local, "seq", scatter_dimension=0, tiled=True),
-    )
+    (proj_parts,) = transfer(
+        7,
+        (
+            "rows",
+            "seq",
+            proj_local.astype(jnp.bfloat16).reshape(
+                shards, proj_local.shape[0] // shards, part_width
+            ),
+        ),
+    )
+    proj_grad = summed(proj_parts)
     return (block_out, proj_grad, value_grad, gate_grad, down_grad, bn_gain_grad, bn_shift_grad)
 
 

time: 503 us -> 199 us (0.40)
  the two profiles are of different devices: /device:TPU:0 before, /device:TPU:13 now
where the time goes in v2:
time: 199 us; the launch traced here: 198 us
  Pallas kernels  145 us (73%)
  other arithmetic  24.5 us (12%)
  matrix products  15.1 us (8%)
  local copies, waits for them, and re-layouts  12.5 us (6%)
    pallas_call x7, Pallas kernels, transfer(): pl.pallas_call(functools.partial(transfer_kernel, plan), out_shape=outs,...  145 us
    reduce_sum x7, other arithmetic, summed(): return jnp.sum(parts.astype(jnp.float32), axis=0)  7.2 us
    dot_general x3, matrix products, contract_cols(): lax.dot_general(left, right, (((1,), (1,)), ((), ())), preferred_element_...  4.53 us
    convert_element_type x1, local copies, waits for them, and re-layouts, body(): proj_local.astype(jnp.bfloat16)  4.1 us

profile of v2, /device:TPU:13, one launch (start us, length us, event | category | flops | bytes accessed | tf_op | source)
XLA Modules:
  0.0 197.9 jit_solution(2628561706649935559)
XLA Ops:
  0.7 0.8 fusion.49
  1.6 0.7 fusion.47
  2.7 2.3 %convolution_convert_fusion.5 = bf16[256,256]{1,0:T(8,128)(2,1)S(1)} fusion(bf16[256,4096]{1,0:T(8,128)(2,1)S(1)} %copy-done, bf16[4096,256]{1,0:T(8,128)(2,1)} %param.12), kind=kOutput, calls=%fused_computation.27 | convolution fusion | flops 536936448 | bytes 4325376 | tf_op jit(solution)/shard_map/dot_general | solution.py:168
  5.0 2.0 gather_fusion
  7.1 0.9 select_select_fusion.refs_0_
  8.3 0.8 broadcast_select_fusion.refs_1_
  9.2 16.3 %shard_map.162 = (bf16[8,64,256]{2,1,0:T(8,128)(2,1)}, bf16[512,1024]{1,0:T(8,128)(2,1)}) custom-call(bf16[8,64,256]{2,1,0:T(8,128)(2,1)} %select_select_fusion.refs_0_, bf16[512,256]{1,0:T(8,128)(2,1)} %broadcast_select_fusion.refs_1_), custom_call_target="tpu_custom_call" | custom-call | tf_op jit(solution)/shard_map/pallas_call | solution.py:86
  25.4 14.1 %shard_map.163 = bf16[512,1024]{1,0:T(8,128)(2,1)} custom-call(bf16[512,256]{1,0:T(8,128)(2,1)} %bitcast.86), custom_call_target="tpu_custom_call" | custom-call | tf_op jit(solution)/shard_map/pallas_call | solution.py:86
  39.5 1.5 convert_reduce_fusion.2
  41.1 1.6 fusion.3
  42.7 1.7 fusion.57
  44.4 0.5 fusion.7
  44.9 0.9 copy-done.6
  45.8 1.2 multiply_multiply_fusion.1
  47.1 0.7 multiply_reduce_fusion.3
  47.8 0.7 maximum_maximum_fusion.1.refs_0_
  48.5 6.0 %shard_map.164 = f32[8,8,256]{2,1,0:T(8,128)} custom-call(f32[8,256]{1,0:T(8,128)} %maximum_maximum_fusion.1.refs_0_), custom_call_target="tpu_custom_call" | custom-call | tf_op jit(solution)/shard_map/pallas_call | solution.py:86
  54.5 0.9 reduce_sum.210
  55.4 2.9 %fusion.53 = (f32[256]{0:T(256)S(1)}, f32[256]{0:T(256)S(1)}, f32[512,256]{1,0:T(8,128)}) fusion(f32[512,256]{1,0:T(8,128)S(1)} %fusion.41, f32[512]{0:T(512)S(1)} %convert_element_type.85, f32[256]{0:T(256)S(1)} %copy-done.23, f32[256]{0:T(256)S(1)} %copy-done.21, bf16[512,1024]{1,0:T(8,128)(2,1)} %get-tuple-element.15, bf16[1024,256]{1,0:T(8,128)(2,1)} %param.18), kind=kOutput, calls=%fused_computation.138 | convolution fusion | flops 270269952 | bytes 2627584 | tf_op jit(solution)/shard_map/dot_general | solution.py:210
  58.3 0.7 maximum_maximum_fusion.2.refs_0_
  59.0 5.9 %shard_map.165 = f32[8,8,256]{2,1,0:T(8,128)} custom-call(f32[8,256]{1,0:T(8,128)} %maximum_maximum_fusion.2.refs_0_), custom_call_target="tpu_custom_call" | custom-call | tf_op jit(solution)/shard_map/pallas_call | solution.py:86
  64.9 0.9 reduce_sum.213
  65.8 1.3 multiply_multiply_fusion
  67.1 0.5 fusion.33
  67.7 0.2 multiply_convert_fusion.3
  67.9 0.5 convolution_convert_fusion.4
  68.4 0.5 convolution_convert_fusion.3
  69.0 0.3 copy-done.22
  69.3 0.6 convolution_convert_fusion.2
  69.9 1.3 pad_maximum_fusion.refs_2_
  71.2 0.5 fusion.63
  71.6 1.1 copy-done.2
  72.8 1.5 fusion.52
  74.4 0.7 maximum_maximum_fusion.refs_1_
  75.1 37.8 %shard_map.166 = (bf16[4,512,256]{2,1,0:T(8,128)(2,1)}, f32[4,8,512]{2,1,0:T(8,128)}, bf16[8,384,256]{2,1,0:T(8,128)(2,1)}) custom-call(bf16[512,1024]{1,0:T(8,128)(2,1)} %get-tuple-element.36.refs_0_, f32[8,512]{1,0:T(8,128)} %maximum_maximum_fusion.refs_1_, bf16[8,384,256]{2,1,0:T(8,128)(2,1)} %pad_maximum_fusion.refs_2_), custom_call_target="tpu_custom_call" | custom-call | tf_op jit(solution)/shard_map/pallas_call | solution.py:86
  112.9 1.4 convert_reduce_fusion.4
  114.3 0.9 reduce_sum.217
  115.2 2.2 %multiply_convert_fusion.1 = bf16[512,256]{1,0:T(8,128)(2,1)} fusion(f32[512,1024]{1,0:T(8,128)} %get-tuple-element.35, s32[]{:T(128)S(6)} %select_n.88, f32[512,256]{1,0:T(8,128)S(1)} %convert_reduce_fusion.4, f32[512]{0:T(512)S(1)} %add_sqrt_fusion, f32[512]{0:T(512)S(1)} %bitcast.118, f32[512]{0:T(512)S(1)} %bitcast.117, f32[512]{0:T(512)S(1)} %convert_element_type.85, ...), kind=kLoop, calls=%fused_computation.80 | loop fusion | flops 1179648 | bytes 1581572 | tf_op jit(solution)/shard_map/convert_element_type | solution.py:249
  117.3 2.5 %convolution_convert_fusion.1.refs_1_ = bf16[512,1024]{1,0:T(8,128)(2,1)} fusion(bf16[1024,256]{1,0:T(8,128)(2,1)} %param.18, f32[512,256]{1,0:T(8,128)S(1)} %copy-done.15, f32[256]{0:T(256)S(1)} %copy-done.23, f32[256]{0:T(256)S(1)} %copy-done.21), kind=kOutput, calls=%fused_computation.16 | convolution fusion | flops 269877248 | bytes 2099200 | tf_op jit(solution)/shard_map/dot_general | solution.py:133
  119.8 15.6 %shard_map.167 = (bf16[8,64,256]{2,1,0:T(8,128)(2,1)}, bf16[4,512,256]{2,1,0:T(8,128)(2,1)}) custom-call(bf16[8,64,256]{2,1,0:T(8,128)(2,1)} %bitcast.87, bf16[512,1024]{1,0:T(8,128)(2,1)} %convolution_convert_fusion.1.refs_1_), custom_call_target="tpu_custom_call" | custom-call | tf_op jit(solution)/shard_map/pallas_call | solution.py:86
  135.7 2.0 gather_fusion.1
  137.7 2.1 %fusion = bf16[4096,256]{0,1:T(8,128)(2,1)} fusion(bf16[256,4096]{1,0:T(8,128)(2,1)S(1)} %copy-done, bf16[256,256]{1,0:T(8,128)(2,1)S(1)} %gather_fusion.1, pred[256]{0:T(512)(128)(4,1)S(1)} %compare_and_fusion.1), kind=kOutput, calls=%fused_computation.3 | convolution fusion | flops 537985024 | bytes 4325632 | tf_op jit(solution)/shard_map/dot_general | solution.py:127
  139.8 4.1 %copy.20 = bf16[4096,256]{1,0:T(8,128)(2,1)} copy(bf16[4096,256]{0,1:T(8,128)(2,1)} %fusion) | data formatting | bytes 4194304 | tf_op jit(solution)/shard_map/convert_element_type | solution.py:273
  143.9 49.1 %shard_map.168 = bf16[8,512,256]{2,1,0:T(8,128)(2,1)} custom-call(bf16[8,512,256]{2,1,0:T(8,128)(2,1)} %bitcast.82), custom_call_target="tpu_custom_call" | custom-call | tf_op jit(solution)/shard_map/pallas_call | solution.py:86
  193.0 2.9 %convert_reduce_fusion = f32[512,256]{1,0:T(8,128)} fusion(bf16[8,512,256]{2,1,0:T(8,128)(2,1)} %shard_map.168), kind=kLoop, calls=%fused_computation.4 | loop fusion | flops 1966080 | bytes 2621440 | tf_op jit(solution)/shard_map/reduce_sum | solution.py:97
  196.0 0.8 multiply_convert_fusion
  196.9 0.2 convert_reduce_fusion.1
  197.1 0.8 fusion.59
  (76 shorter events, 1.6 us)
Async XLA Ops:
  0.6 2.0 %copy-start = (bf16[256,4096]{1,0:T(8,128)(2,1)S(1)}, bf16[256,4096]{1,0:T(8,128)(2,1)}, u32[]{:S(2)}) copy-start(bf16[256,4096]{1,0:T(8,128)(2,1)} %param.11) | copy-start | bytes 6291460
  5.0 3.1 %copy-start.17 = (s32[8,8]{1,0:T(8,128)S(1)}, s32[8,8]{1,0:T(8,128)}, u32[]{:S(2)}) copy-start(s32[8,8]{1,0:T(8,128)} %param.19) | copy-start | bytes 772
  5.0 3.1 %copy-start.18 = (s32[8,8]{1,0:T(8,128)S(1)}, s32[8,8]{1,0:T(8,128)}, u32[]{:S(2)}) copy-start(s32[8,8]{1,0:T(8,128)} %param.20) | copy-start | bytes 772
  5.0 3.3 %copy-start.11 = (bf16[512,256]{1,0:T(8,128)(2,1)S(1)}, bf16[512,256]{1,0:T(8,128)(2,1)}, u32[]{:S(2)}) copy-start(bf16[512,256]{1,0:T(8,128)(2,1)} %param.21) | copy-start | bytes 786436
  39.5 3.2 %copy-start.1 = (bf16[512,1024]{1,0:T(8,128)(2,1)S(1)}, bf16[512,1024]{1,0:T(8,128)(2,1)}, u32[]{:S(2)}) copy-start(bf16[512,1024]{1,0:T(8,128)(2,1)} %shard_map.163) | copy-start | bytes 3145732
  42.7 1.7 copy-start.12
  44.4 2.6 %copy-start.3 = (bf16[512,1024]{1,0:T(8,128)(2,1)}, bf16[512,1024]{1,0:T(8,128)(2,1)S(1)}, u32[]{:S(2)}) copy-start(bf16[512,1024]{1,0:T(8,128)(2,1)S(1)} %get-tuple-element.34) | copy-start | bytes 3145732
  44.4 1.4 copy-start.6
  44.9 2.2 %copy-start.16 = (f32[9,256]{1,0:T(8,128)S(1)}, f32[9,256]{1,0:T(8,128)}, u32[]{:S(2)}) copy-start(f32[9,256]{1,0:T(8,128)} %param.15) | copy-start | bytes 27652
  45.8 9.6 %copy-start.21 = (f32[256]{0:T(256)S(1)}, f32[256]{0:T(256)}, u32[]{:S(2)}) copy-start(f32[256]{0:T(256)} %param.16) | copy-start | bytes 3076
  45.8 9.6 %copy-start.23 = (f32[256]{0:T(256)S(1)}, f32[256]{0:T(256)}, u32[]{:S(2)}) copy-start(f32[256]{0:T(256)} %param.17) | copy-start | bytes 3076
  55.4 2.9 %copy-start.14 = (f32[512,256]{1,0:T(8,128)}, f32[512,256]{1,0:T(8,128)S(1)}, u32[]{:S(2)}) copy-start(f32[512,256]{1,0:T(8,128)S(1)} %fusion.41) | copy-start | bytes 1572868
  65.8 1.9 copy-start.5
  65.8 2.1 %copy-start.19 = (f32[1,256]{1,0:T(1,128)}, f32[1,256]{1,0:T(1,128)S(1)}, u32[]{:S(2)}) copy-start(f32[1,256]{1,0:T(1,128)S(1)} %get-tuple-element.53) | copy-start | bytes 3076
  65.8 2.1 %copy-start.20 = (f32[1,256]{1,0:T(1,128)}, f32[1,256]{1,0:T(1,128)S(1)}, u32[]{:S(2)}) copy-start(f32[1,256]{1,0:T(1,128)S(1)} %get-tuple-element.54) | copy-start | bytes 3076
  65.8 2.1 %copy-start.4 = (bf16[512,1024]{1,0:T(8,128)(2,1)S(1)}, bf16[512,1024]{1,0:T(8,128)(2,1)}, u32[]{:S(2)}) copy-start(bf16[512,1024]{1,0:T(8,128)(2,1)} %copy-done.3) | copy-start | bytes 3145732
  67.9 1.0 copy-start.15
  67.9 1.4 copy-start.22
  69.9 1.3 copy-start.7
  71.2 1.6 copy-start.2
  71.2 1.7 copy-start.13
  193.0 2.9 %copy-start.9 = (bf16[4,512,256]{2,1,0:T(8,128)(2,1)S(1)}, bf16[4,512,256]{2,1,0:T(8,128)(2,1)}, u32[]{:S(2)}) copy-start(bf16[4,512,256]{2,1,0:T(8,128)(2,1)} %get-tuple-element.18) | copy-start | bytes 3145732
  193.0 3.0 %copy-start.10 = (bf16[8,64,256]{2,1,0:T(8,128)(2,1)S(1)}, bf16[8,64,256]{2,1,0:T(8,128)(2,1)}, u32[]{:S(2)}) copy-start(bf16[8,64,256]{2,1,0:T(8,128)(2,1)} %get-tuple-element.14) | copy-start | bytes 786436
  193.0 3.9 %copy-start.8 = (bf16[8,384,256]{2,1,0:T(8,128)(2,1)S(1)}, bf16[8,384,256]{2,1,0:T(8,128)(2,1)}, u32[]{:S(2)}) copy-start(bf16[8,384,256]{2,1,0:T(8,128)(2,1)} %get-tuple-element.20) | copy-start | bytes 4718596

commit v3 on v2

--- a/solution.py
+++ b/solution.py
@@ -9,25 +9,60 @@
 MOST = 64
 
 
+PIECES = 4
+GATHERS = ("columns", "whole", "deal")
+
+
 def source_of(kind, ref, index):
     if kind == "rows":
         return ref.at[index]
     if kind == "split":
         width = ref.shape[1] // lax.axis_size("tp")
         return ref.at[:, pl.ds(pl.multiple_of(index * width, 128), width)]
-    return ref
-
-
-def target_of(kind, ref, index, width):
+    height = ref.shape[0] // lax.axis_size("tp")
+    width = ref.shape[1] // lax.axis_size("seq")
+    begin = pl.multiple_of(lax.axis_index("tp") * height, 16)
+    return ref.at[pl.ds(begin, height), pl.ds(pl.multiple_of(index * width, 128), width)]
+
+
+def pieces_of(kind, ref):
+    return 1 if kind == "whole" and ref.shape[0] < 64 else PIECES
+
+
+def piece_from(source, piece, pieces):
+    height = source.shape[0] // pieces
+    return source.at[pl.ds(piece * height, height)]
+
+
+def piece_in(kind, target, source, index, piece, pieces):
+    height = source.shape[0] // pieces
+    rows = pl.ds(piece * height, height)
     if kind == "columns":
-        return ref.at[:, pl.ds(pl.multiple_of(index * width, 128), width)]
-    return ref.at[index]
+        width = source.shape[1]
+        return target.at[rows, pl.ds(pl.multiple_of(index * width, 128), width)]
+    if kind == "deal":
+        return target.at[rows, index]
+    return target.at[index, rows]
+
+
+def push(source, target, send_sem, recv_sem, axis, peer):
+    copy = pltpu.make_async_remote_copy(
+        src_ref=source,
+        dst_ref=target,
+        send_sem=send_sem,
+        recv_sem=recv_sem,
+        device_id={axis: peer},
+        device_id_type=pl.DeviceIdType.MESH,
+    )
+    copy.start()
+    return copy
 
 
 def transfer_kernel(plan, *refs):
     count = len(plan)
     sources, targets = refs[:count], refs[count : 2 * count]
-    sends, recvs, local_sem = refs[2 * count : 3 * count], refs[3 * count : 4 * count], refs[4 * count]
+    sends, recvs = refs[2 * count : 3 * count], refs[3 * count : 4 * count]
+    local_sem = refs[4 * count]
     barrier = pltpu.get_barrier_semaphore()
     greeted = 0
     for axis in sorted({axis for _, axis in plan}):
@@ -41,28 +76,68 @@
         greeted += size - 1
     pl.semaphore_wait(barrier, greeted)
     copies = []
+    relays = []
     for which, (kind, axis) in enumerate(plan):
         size = lax.axis_size(axis)
         me = lax.axis_index(axis)
         source, target = sources[which], targets[which]
-        width = source.shape[-1]
-        for step in range(1, size):
-            peer = lax.rem(me + step, size)
-            copy = pltpu.make_async_remote_copy(
-                src_ref=source_of(kind, source, peer),
-                dst_ref=target_of(kind, target, me, width),
-                send_sem=sends[which].at[step],
-                recv_sem=recvs[which].at[step],
-                device_id={axis: peer},
-                device_id_type=pl.DeviceIdType.MESH,
+        if kind in GATHERS:
+            pieces = pieces_of(kind, source)
+            partner = me + 1 - 2 * lax.rem(me, 2)
+            for piece in range(pieces):
+                block = piece_from(source, piece, pieces)
+                place = piece_in(kind, target, source, me, piece, pieces)
+                for hop in range(1, size // 2):
+                    slot = hop * pieces + piece
+                    peer = lax.rem(me + 2 * hop, size)
+                    first = push(
+                        block, place, sends[which].at[slot], recvs[which].at[slot], axis, peer
+                    )
+                    relays.append((first, which, hop, piece))
+                copies.append(
+                    push(block, place, sends[which].at[piece], recvs[which].at[piece], axis, partner)
+                )
+            if kind == "columns":
+                width = source.shape[1]
+                home = target.at[:, pl.ds(pl.multiple_of(me * width, 128), width)]
+            elif kind == "deal":
+                home = target.at[:, me]
+            else:
+                home = target.at[me]
+            own = pltpu.make_async_copy(source, home, local_sem.at[which])
+        else:
+            for step in range(1, size):
+                peer = lax.rem(me + step, size)
+                copies.append(
+                    push(
+                        source_of(kind, source, peer),
+                        target.at[me],
+                        sends[which].at[step],
+                        recvs[which].at[step],
+                        axis,
+                        peer,
+                    )
+                )
+            own = pltpu.make_async_copy(
+                source_of(kind, source, me), target.at[me], local_sem.at[which]
             )
-            copy.start()
-            copies.append(copy)
-        own = pltpu.make_async_copy(
-            source_of(kind, source, me), target_of(kind, target, me, width), local_sem.at[which]
-        )
         own.start()
         copies.append(own)
+    for first, which, hop, piece in sorted(relays, key=lambda relay: relay[3]):
+        kind, axis = plan[which]
+        size = lax.axis_size(axis)
+        me = lax.axis_index(axis)
+        pieces = pieces_of(kind, sources[which])
+        origin = lax.rem(me + size - 2 * hop, size)
+        partner = me + 1 - 2 * lax.rem(me, 2)
+        slot = (size // 2 + hop - 1) * pieces + piece
+        first.wait_recv()
+        place = piece_in(kind, targets[which], sources[which], origin, piece, pieces)
+        copies.append(
+            push(place, place, sends[which].at[slot], recvs[which].at[slot], axis, partner)
+        )
+    for first, _, _, _ in relays:
+        first.wait_send()
     for copy in copies:
         copy.wait()
 
@@ -71,18 +146,23 @@
     plan = tuple((kind, axis) for kind, axis, _ in items)
     arrays = [array for _, _, array in items]
     outs = []
+    sems = []
     for kind, axis, array in items:
         size = lax.axis_size(axis)
-        if kind == "rows":
-            shape = array.shape
-        elif kind == "split":
-            shape = (size, array.shape[0], array.shape[1] // size)
+        shape = array.shape
+        if kind == "split":
+            shape = (size, shape[0], shape[1] // size)
         elif kind == "columns":
-            shape = (array.shape[0], array.shape[1] * size)
-        else:
-            shape = (size,) + array.shape
+            shape = (shape[0], shape[1] * size)
+        elif kind == "quarter":
+            shape = (size, shape[0] // lax.axis_size("tp"), shape[1] // size)
+        elif kind == "deal":
+            shape = (shape[0], size) + shape[1:]
+        elif kind == "whole":
+            shape = (size,) + shape
         outs.append(jax.ShapeDtypeStruct(shape, array.dtype))
-    sems = [pltpu.SemaphoreType.DMA((lax.axis_size(axis),)) for _, axis in plan]
+        slots = size * pieces_of(kind, array) if kind in GATHERS else size
+        sems.append(pltpu.SemaphoreType.DMA((slots,)))
     return pl.pallas_call(
         functools.partial(transfer_kernel, plan),
         out_shape=outs,
@@ -154,22 +234,24 @@
     own_rows = subsampled.shape[0]
     part_width = proj_weight.shape[1]
     count = float(own_rows * shards)
-    clip_lens = lax.dynamic_slice_in_dim(clip_frames, seq_index, 1, 0)[0]
-    clip_targets = lax.dynamic_slice_in_dim(clip_dest, seq_index, 1, 0)[0]
     shard_ids = jnp.arange(shards, dtype=jnp.int32)
     earlier = shard_ids[None, :] < shard_ids[:, None]
-    offsets = jnp.sum(jnp.where(earlier, clip_lens[None, :], 0), axis=1)
-    match = clip_targets[None, :] == shard_ids[:, None]
-    starts = jnp.sum(jnp.where(match, offsets[None, :], 0), axis=1)
-    lengths = jnp.sum(jnp.where(match, clip_lens[None, :], 0), axis=1)
+    offsets = jnp.sum(jnp.where(earlier[None], clip_frames[:, None, :], 0), axis=2)
+    row_ids = jnp.arange(own_rows, dtype=jnp.int32)[None, :, None]
+    begins = offsets[:, None, :]
+    inside = (row_ids >= begins) & (row_ids < begins + clip_frames[:, None, :])
+    slot_of_row = jnp.sum(
+        jnp.where(inside, clip_dest[:, None, :] * MOST + row_ids - begins, 0), axis=2
+    )
+    slot_ids = jnp.arange(shards * MOST, dtype=jnp.int32)
     frame_pos = jnp.arange(MOST, dtype=jnp.int32)
-    source_rows = jnp.minimum(starts[:, None] + frame_pos[None, :], own_rows - 1).reshape(-1)
-    send_valid = (frame_pos[None, :] < lengths[:, None]).reshape(-1, 1)
+    own_slots = lax.dynamic_slice_in_dim(slot_of_row, seq_index, 1, 0)
+    to_slots = (slot_ids[:, None] == own_slots).astype(jnp.bfloat16)
     projected = jnp.dot(subsampled, proj_weight, preferred_element_type=jnp.float32).astype(
         jnp.bfloat16
     )
-    outgoing = jnp.where(
-        send_valid, jnp.take(projected, source_rows, axis=0), jnp.zeros((), jnp.bfloat16)
+    outgoing = jnp.dot(to_slots, projected, preferred_element_type=jnp.float32).astype(
+        jnp.bfloat16
     )
     incoming = clip_dest == seq_index
     in_lengths = jnp.sum(jnp.where(incoming, clip_frames, 0), axis=1)
@@ -182,7 +264,9 @@
         ("columns", "tp", grad_out),
     )
     hidden_part = arrived.reshape(shards * MOST, part_width)
-    (hidden_full,) = transfer(2, ("columns", "tp", hidden_part))
+    hidden_full, quarter = transfer(
+        2, ("columns", "tp", hidden_part), ("quarter", "seq", subsampled)
+    )
     hidden32 = hidden_full.astype(jnp.float32)
     centred = hidden32 - jnp.mean(hidden32, axis=1, keepdims=True)
     sigma = jnp.sqrt(jnp.mean(centred * centred, axis=1, keepdims=True) + 1e-05)
@@ -237,10 +321,11 @@
         ],
         axis=1,
     )
-    normed_parts, row_parts, weight_blocks = transfer(
+    normed_parts, row_parts, gathered_sub, weight_blocks = transfer(
         5,
         ("split", "tp", normed_terms.astype(jnp.bfloat16)),
         ("whole", "tp", row_sums),
+        ("whole", "tp", quarter.reshape(-1, quarter.shape[2])),
         ("rows", "seq", weight_parts),
     )
     row_means = (summed(row_parts) / width_all).T
@@ -249,33 +334,30 @@
     grad_packed = ((grad_out.astype(jnp.float32) + grad_hidden) * mask).astype(jnp.bfloat16)
     returned, mixed_parts = transfer(
         6,
-        ("rows", "seq", grad_packed.reshape(shards, MOST, part_width)),
+        ("deal", "seq", grad_packed.reshape(shards, MOST, part_width)),
         ("split", "tp", mixed_local),
     )
     block_out = ((hidden_part.astype(jnp.float32) + summed(mixed_parts)) * mask).astype(
         jnp.bfloat16
     )
     value_grad, gate_grad, down_grad = jnp.split(summed(weight_blocks), 3, axis=0)
-    row_ids = jnp.arange(own_rows, dtype=jnp.int32)
-    clip_ends = offsets + clip_lens
-    clip_of_row = jnp.sum((clip_ends[None, :] <= row_ids[:, None]).astype(jnp.int32), axis=1)
-    row_match = clip_of_row[:, None] == shard_ids[None, :]
-    row_start = jnp.sum(jnp.where(row_match, offsets[None, :], 0), axis=1)
-    row_target = jnp.sum(jnp.where(row_match, clip_targets[None, :], 0), axis=1)
-    positions = row_target * MOST + row_ids - row_start
-    grad_proj = jnp.take(returned.reshape(shards * MOST, part_width), positions, axis=0)
-    proj_local = contract_rows(subsampled, grad_proj)
-    (proj_parts,) = transfer(
-        7,
-        (
-            "rows",
-            "seq",
-            proj_local.astype(jnp.bfloat16).reshape(
-                shards, proj_local.shape[0] // shards, part_width
-            ),
-        ),
-    )
-    proj_grad = summed(proj_parts)
+    returned = returned.reshape(shards, shards * MOST, part_width)
+    if shards <= 8:
+        to_rows = (slot_of_row[:, :, None] == slot_ids[None, None, :]).astype(jnp.bfloat16)
+        grad_proj = lax.dot_general(
+            to_rows,
+            returned,
+            (((2,), (1,)), ((0,), (0,))),
+            preferred_element_type=jnp.float32,
+        ).astype(jnp.bfloat16)
+    else:
+        grad_proj = jnp.take_along_axis(returned, slot_of_row[:, :, None], axis=1)
+    ranks = lax.axis_size("tp")
+    grad_proj = grad_proj.reshape(shards, ranks, own_rows // ranks, part_width)
+    grad_proj = jnp.swapaxes(grad_proj, 0, 1).reshape(shards * own_rows, part_width)
+    proj_grad = contract_rows(
+        gathered_sub.reshape(shards * own_rows, gathered_sub.shape[2]), grad_proj
+    )
     return (block_out, proj_grad, value_grad, gate_grad, down_grad, bn_gain_grad, bn_shift_grad)
 
 

time: 199 us -> 167 us (0.84)
  the two profiles are of different devices: /device:TPU:13 before, /device:TPU:0 now
where the time goes in v3:
time: 167 us; the launch traced here: 164 us
  Pallas kernels  118 us (71%)
  other arithmetic  21.2 us (13%)
  matrix products  18.1 us (11%)
  local copies, waits for them, and re-layouts  5.61 us (3%)
    pallas_call x6, Pallas kernels, transfer(): pl.pallas_call(functools.partial(transfer_kernel, plan), out_shape=outs,...  118 us
    unnamed x48, local copies, waits for them, and re-layouts  4.56 us
    dot_general x3, matrix products, contract_cols(): lax.dot_general(left, right, (((1,), (1,)), ((), ())), preferred_element_...  4.5 us
    reduce_sum x6, other arithmetic, summed(): return jnp.sum(parts.astype(jnp.float32), axis=0)  4.38 us
    dot_general x1, matrix products, body(): jnp.dot(to_slots, projected, preferred_element_type=jnp.float32)  3.37 us

profile of v3, /device:TPU:0, one launch (start us, length us, event | category | flops | bytes accessed | tf_op | source)
XLA Modules:
  0.0 164.4 jit_solution(3353606070552917238)
XLA Ops:
  0.7 1.0 select_reduce_fusion.1
  1.7 0.8 select_reduce_fusion.2
  2.5 0.1 select_reduce_fusion
  2.7 3.4 %convolution_convert_fusion.4 = bf16[512,256]{1,0:T(8,128)(2,1)} fusion(bf16[256,4096]{1,0:T(8,128)(2,1)} %refs_1_.1, bf16[4096,256]{1,0:T(8,128)(2,1)S(1)} %copy-done, s32[256]{0:T(256)S(1)} %bitcast.119), kind=kOutput, calls=%fused_computation.26 | convolution fusion | flops 604307456 | bytes 4457472 | tf_op jit(solution)/shard_map/dot_general | solution.py:253
  6.2 0.8 broadcast_select_fusion.refs_1_
  7.1 16.5 %shard_map.162 = (bf16[8,64,256]{2,1,0:T(8,128)(2,1)}, bf16[512,1024]{1,0:T(8,128)(2,1)}) custom-call(bf16[8,64,256]{2,1,0:T(8,128)(2,1)} %bitcast.85, bf16[512,256]{1,0:T(8,128)(2,1)} %broadcast_select_fusion.refs_1_), custom_call_target="tpu_custom_call" | custom-call | tf_op jit(solution)/shard_map/pallas_call | solution.py:166
  23.6 13.1 %shard_map.163 = (bf16[512,1024]{1,0:T(8,128)(2,1)}, bf16[8,64,512]{2,1,0:T(8,128)(2,1)}) custom-call(bf16[512,256]{1,0:T(8,128)(2,1)} %bitcast.79, bf16[256,4096]{1,0:T(8,128)(2,1)} %refs_1_.1), custom_call_target="tpu_custom_call" | custom-call | tf_op jit(solution)/shard_map/pallas_call | solution.py:166
  36.6 1.5 convert_reduce_fusion.1
  38.2 1.6 fusion.3
  39.8 1.7 %fusion.54 = (bf16[512,1024]{1,0:T(8,128)(2,1)S(1)}, f32[512,1024]{1,0:T(8,128)}) fusion(f32[512]{0:T(512)S(1)} %add_sqrt_fusion, f32[512]{0:T(512)S(1)} %broadcast_multiply_fusion.1, bf16[512,1024]{1,0:T(8,128)(2,1)S(1)} %copy-done.2), kind=kLoop, calls=%fused_computation.118 | loop fusion | flops 2097152 | bytes 4198400 | tf_op jit(solution)/shard_map/convert_element_type | solution.py:274
  41.5 0.5 fusion.9
  42.0 0.9 copy-done.7
  42.9 1.2 multiply_multiply_fusion.1
  44.2 0.7 multiply_reduce_fusion.3
  44.9 0.7 maximum_maximum_fusion.1.refs_0_
  45.6 10.9 %shard_map.164 = f32[8,8,256]{2,1,0:T(8,128)} custom-call(f32[8,256]{1,0:T(8,128)} %maximum_maximum_fusion.1.refs_0_), custom_call_target="tpu_custom_call" | custom-call | tf_op jit(solution)/shard_map/pallas_call | solution.py:166
  56.5 0.9 reduce_sum.160
  57.5 2.9 %fusion.50 = (f32[256]{0:T(256)S(1)}, f32[256]{0:T(256)S(1)}, f32[512,256]{1,0:T(8,128)}) fusion(f32[512,256]{1,0:T(8,128)S(1)} %fusion.43, f32[512]{0:T(512)S(1)} %convert_element_type.82, f32[256]{0:T(256)S(1)} %copy-done.23, f32[256]{0:T(256)S(1)} %copy-done.21, bf16[512,1024]{1,0:T(8,128)(2,1)} %get-tuple-element.19, bf16[1024,256]{1,0:T(8,128)(2,1)} %param.18), kind=kOutput, calls=%fused_computation.116 | convolution fusion | flops 270269952 | bytes 2627584 | tf_op jit(solution)/shard_map/dot_general | solution.py:294
  60.3 0.7 maximum_maximum_fusion.2.refs_0_
  61.0 9.5 %shard_map.165 = f32[8,8,256]{2,1,0:T(8,128)} custom-call(f32[8,256]{1,0:T(8,128)} %maximum_maximum_fusion.2.refs_0_), custom_call_target="tpu_custom_call" | custom-call | tf_op jit(solution)/shard_map/pallas_call | solution.py:166
  70.5 0.9 reduce_sum.163
  71.4 1.3 multiply_multiply_fusion
  72.7 0.5 fusion.35
  73.3 0.2 multiply_convert_fusion.3
  73.6 0.5 convolution_convert_fusion.3
  74.0 0.5 convolution_convert_fusion.2
  74.6 0.3 copy-done.22
  74.9 0.6 convolution_convert_fusion.1
  75.5 1.3 pad_maximum_fusion.refs_3_
  76.8 0.5 fusion.60
  77.3 1.1 copy-done.1
  78.5 1.5 fusion.49
  80.0 0.7 maximum_maximum_fusion.refs_1_
  80.7 35.9 %shard_map.166 = (bf16[4,512,256]{2,1,0:T(8,128)(2,1)}, f32[4,8,512]{2,1,0:T(8,128)}, bf16[4,512,512]{2,1,0:T(8,128)(2,1)}, bf16[8,384,256]{2,1,0:T(8,128)(2,1)}) custom-call(bf16[512,1024]{1,0:T(8,128)(2,1)} %get-tuple-element.38.refs_0_, f32[8,512]{1,0:T(8,128)} %maximum_maximum_fusion.refs_1_, bf16[512,512]{1,0:T(8,128)(2,1)} %bitcast.81, ...), custom_call_target="tpu_custom_call" | custom-call | tf_op jit(solution)/shard_map/pallas_call | solution.py:166
  116.7 1.5 convert_reduce_fusion.3
  118.1 0.9 reduce_sum.167
  119.0 2.2 %multiply_convert_fusion.1 = bf16[512,256]{1,0:T(8,128)(2,1)} fusion(f32[512,1024]{1,0:T(8,128)} %get-tuple-element.37, s32[]{:T(128)S(6)} %select_n.27, f32[512,256]{1,0:T(8,128)S(1)} %convert_reduce_fusion.3, f32[512]{0:T(512)S(1)} %add_sqrt_fusion, f32[512]{0:T(512)S(1)} %bitcast.111, f32[512]{0:T(512)S(1)} %bitcast.110, f32[512]{0:T(512)S(1)} %convert_element_type.82, ...), kind=kLoop, calls=%fused_computation.80 | loop fusion | flops 1179648 | bytes 1581572 | tf_op jit(solution)/shard_map/convert_element_type | solution.py:334
  121.2 2.5 %convolution_convert_fusion.refs_1_ = bf16[512,1024]{1,0:T(8,128)(2,1)} fusion(bf16[1024,256]{1,0:T(8,128)(2,1)} %param.18, f32[512,256]{1,0:T(8,128)S(1)} %copy-done.17, f32[256]{0:T(256)S(1)} %copy-done.23, f32[256]{0:T(256)S(1)} %copy-done.21), kind=kOutput, calls=%fused_computation.15 | convolution fusion | flops 269877248 | bytes 2099200 | tf_op jit(solution)/shard_map/dot_general | solution.py:213
  123.7 32.5 %shard_map.167 = (bf16[8,8,64,256]{3,2,1,0:T(8,128)(2,1)}, bf16[4,512,256]{2,1,0:T(8,128)(2,1)}) custom-call(bf16[8,64,256]{2,1,0:T(8,128)(2,1)} %bitcast.80, bf16[512,1024]{1,0:T(8,128)(2,1)} %convolution_convert_fusion.refs_1_), custom_call_target="tpu_custom_call" | custom-call | tf_op jit(solution)/shard_map/pallas_call | solution.py:166
  156.2 2.6 %fusion.5 = bf16[8,256,256]{2,1,0:T(8,128)(2,1)S(1)} fusion(bf16[8,512,256]{2,1,0:T(8,128)(2,1)} %bitcast.122, s32[8,256]{1,0:T(8,128)S(1)} %select_reduce_fusion), kind=kOutput, calls=%fused_computation.14 | convolution fusion | flops 538443776 | bytes 3153920 | tf_op jit(solution)/shard_map/dot_general | solution.py:347
  158.8 0.1 copy.19
  159.0 1.5 copy-done.5
  160.4 1.5 fusion.61
  162.0 0.1 convert_reduce_fusion.2
  162.1 0.8 multiply_convert_fusion
  163.0 0.5 copy-done.9
  163.5 0.2 convert_reduce_fusion
  163.7 0.8 fusion.56
  (60 shorter events, 0.6 us)
Async XLA Ops:
  0.6 2.0 %copy-start = (bf16[4096,256]{1,0:T(8,128)(2,1)S(1)}, bf16[4096,256]{1,0:T(8,128)(2,1)}, u32[]{:S(2)}) copy-start(bf16[4096,256]{1,0:T(8,128)(2,1)} %param.12) | copy-start | bytes 6291460
  2.7 3.5 %copy-start.12 = (bf16[512,256]{1,0:T(8,128)(2,1)S(1)}, bf16[512,256]{1,0:T(8,128)(2,1)}, u32[]{:S(2)}) copy-start(bf16[512,256]{1,0:T(8,128)(2,1)} %param.21) | copy-start | bytes 786436
  36.6 3.2 %copy-start.2 = (bf16[512,1024]{1,0:T(8,128)(2,1)S(1)}, bf16[512,1024]{1,0:T(8,128)(2,1)}, u32[]{:S(2)}) copy-start(bf16[512,1024]{1,0:T(8,128)(2,1)} %get-tuple-element.18) | copy-start | bytes 3145732
  39.8 1.7 %copy-start.13 = (bf16[1024,256]{1,0:T(8,128)(2,1)S(1)}, bf16[1024,256]{1,0:T(8,128)(2,1)}, u32[]{:S(2)}) copy-start(bf16[1024,256]{1,0:T(8,128)(2,1)} %param.14) | copy-start | bytes 1572868
  41.5 2.6 %copy-start.3 = (bf16[512,1024]{1,0:T(8,128)(2,1)}, bf16[512,1024]{1,0:T(8,128)(2,1)S(1)}, u32[]{:S(2)}) copy-start(bf16[512,1024]{1,0:T(8,128)(2,1)S(1)} %get-tuple-element.36) | copy-start | bytes 3145732
  41.5 1.4 copy-start.7
  42.0 2.2 %copy-start.18 = (f32[9,256]{1,0:T(8,128)S(1)}, f32[9,256]{1,0:T(8,128)}, u32[]{:S(2)}) copy-start(f32[9,256]{1,0:T(8,128)} %param.15) | copy-start | bytes 27652
  42.9 14.5 %copy-start.21 = (f32[256]{0:T(256)S(1)}, f32[256]{0:T(256)}, u32[]{:S(2)}) copy-start(f32[256]{0:T(256)} %param.16) | copy-start | bytes 3076
  42.9 14.6 %copy-start.23 = (f32[256]{0:T(256)S(1)}, f32[256]{0:T(256)}, u32[]{:S(2)}) copy-start(f32[256]{0:T(256)} %param.17) | copy-start | bytes 3076
  57.5 2.9 %copy-start.15 = (f32[512,256]{1,0:T(8,128)}, f32[512,256]{1,0:T(8,128)S(1)}, u32[]{:S(2)}) copy-start(f32[512,256]{1,0:T(8,128)S(1)} %fusion.43) | copy-start | bytes 1572868
  71.4 1.9 %copy-start.6 = (f32[512,256]{1,0:T(8,128)S(1)}, f32[512,256]{1,0:T(8,128)}, u32[]{:S(2)}) copy-start(f32[512,256]{1,0:T(8,128)} %get-tuple-element.64) | copy-start | bytes 1572868
  71.4 2.1 %copy-start.19 = (f32[1,256]{1,0:T(1,128)}, f32[1,256]{1,0:T(1,128)S(1)}, u32[]{:S(2)}) copy-start(f32[1,256]{1,0:T(1,128)S(1)} %get-tuple-element.55) | copy-start | bytes 3076
  71.4 2.1 %copy-start.20 = (f32[1,256]{1,0:T(1,128)}, f32[1,256]{1,0:T(1,128)S(1)}, u32[]{:S(2)}) copy-start(f32[1,256]{1,0:T(1,128)S(1)} %get-tuple-element.56) | copy-start | bytes 3076
  71.4 2.1 %copy-start.4 = (bf16[512,1024]{1,0:T(8,128)(2,1)S(1)}, bf16[512,1024]{1,0:T(8,128)(2,1)}, u32[]{:S(2)}) copy-start(bf16[512,1024]{1,0:T(8,128)(2,1)} %copy-done.3) | copy-start | bytes 3145732
  73.5 1.0 copy-start.16
  73.5 1.4 copy-start.22
  75.5 1.3 copy-start.8
  76.8 1.6 copy-start.1
  76.8 1.7 %copy-start.14 = (bf16[1024,256]{1,0:T(8,128)(2,1)S(1)}, bf16[1024,256]{1,0:T(8,128)(2,1)}, u32[]{:S(2)}) copy-start(bf16[1024,256]{1,0:T(8,128)(2,1)} %param.14) | copy-start | bytes 1572868
  116.7 4.5 %copy-start.17 = (f32[512,256]{1,0:T(8,128)S(1)}, f32[512,256]{1,0:T(8,128)}, u32[]{:S(2)}) copy-start(f32[512,256]{1,0:T(8,128)} %copy-done.15) | copy-start | bytes 1572868
  158.8 1.6 copy-start.5
  159.0 3.0 %copy-start.10 = (bf16[4,512,256]{2,1,0:T(8,128)(2,1)S(1)}, bf16[4,512,256]{2,1,0:T(8,128)(2,1)}, u32[]{:S(2)}) copy-start(bf16[4,512,256]{2,1,0:T(8,128)(2,1)} %get-tuple-element.23) | copy-start | bytes 3145732
  160.4 1.7 %copy-start.11 = (bf16[8,64,256]{2,1,0:T(8,128)(2,1)S(1)}, bf16[8,64,256]{2,1,0:T(8,128)(2,1)}, u32[]{:S(2)}) copy-start(bf16[8,64,256]{2,1,0:T(8,128)(2,1)} %get-tuple-element.17) | copy-start | bytes 786436
  162.0 1.5 copy-start.9

commit v4 on v3

--- a/solution.py
+++ b/solution.py
@@ -16,6 +16,8 @@
 def source_of(kind, ref, index):
     if kind == "rows":
         return ref.at[index]
+    if kind == "small":
+        return ref
     if kind == "split":
         width = ref.shape[1] // lax.axis_size("tp")
         return ref.at[:, pl.ds(pl.multiple_of(index * width, 128), width)]
@@ -26,7 +28,7 @@
 
 
 def pieces_of(kind, ref):
-    return 1 if kind == "whole" and ref.shape[0] < 64 else PIECES
+    return PIECES
 
 
 def piece_from(source, piece, pieces):
@@ -58,14 +60,10 @@
     return copy
 
 
-def transfer_kernel(plan, *refs):
-    count = len(plan)
-    sources, targets = refs[:count], refs[count : 2 * count]
-    sends, recvs = refs[2 * count : 3 * count], refs[3 * count : 4 * count]
-    local_sem = refs[4 * count]
+def greet(axes):
     barrier = pltpu.get_barrier_semaphore()
     greeted = 0
-    for axis in sorted({axis for _, axis in plan}):
+    for axis in axes:
         size = lax.axis_size(axis)
         me = lax.axis_index(axis)
         for step in range(1, size):
@@ -75,69 +73,131 @@
             )
         greeted += size - 1
     pl.semaphore_wait(barrier, greeted)
+
+
+def partner_of(me):
+    return me + 1 - 2 * lax.rem(me, 2)
+
+
+def start_gather(kind, axis, source, target, send, recv, local):
+    size = lax.axis_size(axis)
+    me = lax.axis_index(axis)
+    pieces = pieces_of(kind, source)
+    copies, relays = [], []
+    for piece in range(pieces):
+        block = piece_from(source, piece, pieces)
+        place = piece_in(kind, target, source, me, piece, pieces)
+        for hop in range(1, size // 2):
+            slot = hop * pieces + piece
+            peer = lax.rem(me + 2 * hop, size)
+            first = push(block, place, send.at[slot], recv.at[slot], axis, peer)
+            relays.append((piece, first, hop, (kind, axis, source, target, send, recv)))
+        copies.append(push(block, place, send.at[piece], recv.at[piece], axis, partner_of(me)))
+    if kind == "columns":
+        width = source.shape[1]
+        home = target.at[:, pl.ds(pl.multiple_of(me * width, 128), width)]
+    elif kind == "deal":
+        home = target.at[:, me]
+    else:
+        home = target.at[me]
+    own = pltpu.make_async_copy(source, home, local)
+    own.start()
+    copies.append(own)
+    return copies, relays
+
+
+def relay_all(relays):
     copies = []
-    relays = []
-    for which, (kind, axis) in enumerate(plan):
+    for piece, first, hop, (kind, axis, source, target, send, recv) in sorted(
+        relays, key=lambda relay: relay[0]
+    ):
         size = lax.axis_size(axis)
         me = lax.axis_index(axis)
-        source, target = sources[which], targets[which]
-        if kind in GATHERS:
-            pieces = pieces_of(kind, source)
-            partner = me + 1 - 2 * lax.rem(me, 2)
-            for piece in range(pieces):
-                block = piece_from(source, piece, pieces)
-                place = piece_in(kind, target, source, me, piece, pieces)
-                for hop in range(1, size // 2):
-                    slot = hop * pieces + piece
-                    peer = lax.rem(me + 2 * hop, size)
-                    first = push(
-                        block, place, sends[which].at[slot], recvs[which].at[slot], axis, peer
-                    )
-                    relays.append((first, which, hop, piece))
-                copies.append(
-                    push(block, place, sends[which].at[piece], recvs[which].at[piece], axis, partner)
-                )
-            if kind == "columns":
-                width = source.shape[1]
-                home = target.at[:, pl.ds(pl.multiple_of(me * width, 128), width)]
-            elif kind == "deal":
-                home = target.at[:, me]
-            else:
-                home = target.at[me]
-            own = pltpu.make_async_copy(source, home, local_sem.at[which])
-        else:
-            for step in range(1, size):
-                peer = lax.rem(me + step, size)
-                copies.append(
-                    push(
-                        source_of(kind, source, peer),
-                        target.at[me],
-                        sends[which].at[step],
-                        recvs[which].at[step],
-                        axis,
-                        peer,
-                    )
-                )
-            own = pltpu.make_async_copy(
-                source_of(kind, source, me), target.at[me], local_sem.at[which]
-            )
-        own.start()
-        copies.append(own)
-    for first, which, hop, piece in sorted(relays, key=lambda relay: relay[3]):
-        kind, axis = plan[which]
-        size = lax.axis_size(axis)
-        me = lax.axis_index(axis)
-        pieces = pieces_of(kind, sources[which])
+        pieces = pieces_of(kind, source)
         origin = lax.rem(me + size - 2 * hop, size)
-        partner = me + 1 - 2 * lax.rem(me, 2)
         slot = (size // 2 + hop - 1) * pieces + piece
         first.wait_recv()
-        place = piece_in(kind, targets[which], sources[which], origin, piece, pieces)
+        place = piece_in(kind, target, source, origin, piece, pieces)
+        copies.append(push(place, place, send.at[slot], recv.at[slot], axis, partner_of(me)))
+    for _, first, _, _ in relays:
+        first.wait_send()
+    return copies
+
+
+def start_direct(kind, axis, source, target, send, recv, local):
+    size = lax.axis_size(axis)
+    me = lax.axis_index(axis)
+    copies = []
+    for step in range(1, size):
+        peer = lax.rem(me + step, size)
+        block = source_of(kind, source, peer)
+        copies.append(push(block, target.at[me], send.at[step], recv.at[step], axis, peer))
+    own = pltpu.make_async_copy(source_of(kind, source, me), target.at[me], local)
+    own.start()
+    copies.append(own)
+    return copies
+
+
+def start_reduce(axis, source, landing, send, recv):
+    half = lax.axis_size(axis) // 2
+    me = lax.axis_index(axis)
+    partner = partner_of(me)
+    copies = []
+    for step in range(half):
+        line = lax.rem(me // 2 + 1 + step, half)
+        block = source.at[2 * line + lax.rem(partner, 2)]
         copies.append(
-            push(place, place, sends[which].at[slot], recvs[which].at[slot], axis, partner)
+            push(block, landing.at[step], send.at[step], recv.at[step], axis, partner)
         )
-    for first, _, _, _ in relays:
-        first.wait_send()
+    return copies
+
+
+def finish_reduce(axis, firsts, source, landing, partial, target, send, recv, local):
+    half = lax.axis_size(axis) // 2
+    me = lax.axis_index(axis)
+    copies = []
+    for step in range(half):
+        line = lax.rem(me // 2 + 1 + step, half)
+        peer = 2 * line + lax.rem(me, 2)
+        firsts[step].wait()
+        both = source[peer].astype(jnp.float32) + landing[step].astype(jnp.float32)
+        partial[step] = both.astype(partial.dtype)
+        place = target.at[me // 2]
+        if step < half - 1:
+            slot = half + step
+            copies.append(
+                push(partial.at[step], place, send.at[slot], recv.at[slot], axis, peer)
+            )
+        else:
+            own = pltpu.make_async_copy(partial.at[step], place, local)
+            own.start()
+            copies.append(own)
+    return copies
+
+
+def transfer_kernel(plan, *refs):
+    count = len(plan)
+    sources, targets = refs[:count], refs[count : 2 * count]
+    sends, recvs = refs[2 * count : 3 * count], refs[3 * count : 4 * count]
+    local_sem = refs[4 * count]
+    rooms = refs[4 * count + 1 :]
+    greet(sorted({axis for _, axis in plan}))
+    copies, relays, firsts, reduced = [], [], [], None
+    for which, (kind, axis) in enumerate(plan):
+        source, target = sources[which], targets[which]
+        send, recv, local = sends[which], recvs[which], local_sem.at[which]
+        if kind == "reduce":
+            firsts = start_reduce(axis, source, rooms[0], send, recv)
+            reduced = (axis, firsts, source, rooms[0], rooms[1], target, send, recv, local)
+        elif kind in GATHERS:
+            started, waiting = start_gather(kind, axis, source, target, send, recv, local)
+            copies += started
+            relays += waiting
+        else:
+            copies += start_direct(kind, axis, source, target, send, recv, local)
+    if reduced is not None:
+        copies += finish_reduce(*reduced)
+    copies += relay_all(relays)
     for copy in copies:
         copy.wait()
 
@@ -145,8 +205,7 @@
 def transfer(number, *items):
     plan = tuple((kind, axis) for kind, axis, _ in items)
     arrays = [array for _, _, array in items]
-    outs = []
-    sems = []
+    outs, sems, specs, rooms = [], [], [], []
     for kind, axis, array in items:
         size = lax.axis_size(axis)
         shape = array.shape
@@ -156,21 +215,92 @@
             shape = (shape[0], shape[1] * size)
         elif kind == "quarter":
             shape = (size, shape[0] // lax.axis_size("tp"), shape[1] // size)
-        elif kind == "deal":
-            shape = (shape[0], size) + shape[1:]
-        elif kind == "whole":
+        elif kind == "reduce":
+            shape = (size // 2,) + shape[1:]
+            rooms = [pltpu.VMEM(shape, array.dtype)] * 2
+        elif kind in ("whole", "small"):
             shape = (size,) + shape
         outs.append(jax.ShapeDtypeStruct(shape, array.dtype))
+        specs.append(pl.BlockSpec(memory_space=pltpu.VMEM if kind == "reduce" else pl.ANY))
         slots = size * pieces_of(kind, array) if kind in GATHERS else size
         sems.append(pltpu.SemaphoreType.DMA((slots,)))
     return pl.pallas_call(
         functools.partial(transfer_kernel, plan),
         out_shape=outs,
-        in_specs=[pl.BlockSpec(memory_space=pl.ANY)] * len(arrays),
+        in_specs=specs,
         out_specs=[pl.BlockSpec(memory_space=pl.ANY)] * len(arrays),
-        scratch_shapes=sems + sems + [pltpu.SemaphoreType.DMA((len(plan),))],
+        scratch_shapes=sems + sems + [pltpu.SemaphoreType.DMA((len(plan),))] + rooms,
         compiler_params=pltpu.CompilerParams(collective_id=number, has_side_effects=True),
     )(*arrays)
+
+
+def return_kernel(
+    packed,
+    to_rows,
+    mixed,
+    gathered,
+    mixed_parts,
+    landing,
+    owned,
+    packed_send,
+    packed_recv,
+    mixed_send,
+    mixed_recv,
+    owned_send,
+    owned_recv,
+    local_sem,
+):
+    greet(("seq", "tp"))
+    arrivals = start_direct(
+        "rows", "seq", packed, landing, packed_send, packed_recv, local_sem.at[0]
+    )
+    copies = start_direct("split", "tp", mixed, mixed_parts, mixed_send, mixed_recv, local_sem.at[1])
+    for copy in arrivals:
+        copy.wait()
+    frames = landing[...].reshape(-1, landing.shape[2])
+    rows = jnp.dot(to_rows[...], frames, preferred_element_type=jnp.float32)
+    owned[...] = rows.astype(owned.dtype).reshape(owned.shape)
+    started, relays = start_gather(
+        "deal", "seq", owned, gathered, owned_send, owned_recv, local_sem.at[2]
+    )
+    copies += started
+    copies += relay_all(relays)
+    for copy in copies:
+        copy.wait()
+
+
+def send_back(number, packed, to_rows, mixed):
+    shards = lax.axis_size("seq")
+    ranks = lax.axis_size("tp")
+    height = to_rows.shape[0] // ranks
+    width = packed.shape[2]
+    owned = (ranks, height, width)
+    dma = pltpu.SemaphoreType.DMA
+    return pl.pallas_call(
+        return_kernel,
+        out_shape=[
+            jax.ShapeDtypeStruct((ranks, shards, height, width), packed.dtype),
+            jax.ShapeDtypeStruct((ranks, mixed.shape[0], mixed.shape[1] // ranks), mixed.dtype),
+        ],
+        in_specs=[
+            pl.BlockSpec(memory_space=pl.ANY),
+            pl.BlockSpec(memory_space=pltpu.VMEM),
+            pl.BlockSpec(memory_space=pl.ANY),
+        ],
+        out_specs=[pl.BlockSpec(memory_space=pl.ANY)] * 2,
+        scratch_shapes=[
+            pltpu.VMEM(packed.shape, packed.dtype),
+            pltpu.VMEM(owned, packed.dtype),
+            dma((shards,)),
+            dma((shards,)),
+            dma((ranks,)),
+            dma((ranks,)),
+            dma((shards * PIECES,)),
+            dma((shards * PIECES,)),
+            dma((3,)),
+        ],
+        compiler_params=pltpu.CompilerParams(collective_id=number, has_side_effects=True),
+    )(packed, to_rows, mixed)
 
 
 def summed(parts):
@@ -278,7 +408,7 @@
     glu = value_pre * gate_sig * mask
     conv = depthwise(glu.reshape(shards, MOST, part_width), conv_kernel).reshape(-1, part_width)
     (conv_parts,) = transfer(
-        3, ("whole", "seq", stacked(jnp.sum(conv * mask, axis=0), jnp.sum(conv * conv * mask, axis=0)))
+        3, ("small", "seq", stacked(jnp.sum(conv * mask, axis=0), jnp.sum(conv * conv * mask, axis=0)))
     )
     conv_sums = summed(conv_parts)
     conv_total, square_total = conv_sums[0], conv_sums[1]
@@ -294,7 +424,7 @@
     grad_swish = jnp.dot(grad_full, down_weight, preferred_element_type=jnp.float32)
     grad_bn = grad_swish * bn_sig * (1.0 + batch_normed * (1.0 - bn_sig)) * mask
     (bn_parts,) = transfer(
-        4, ("whole", "seq", stacked(jnp.sum(grad_bn, axis=0), jnp.sum(grad_bn * bn_hat, axis=0)))
+        4, ("small", "seq", stacked(jnp.sum(grad_bn, axis=0), jnp.sum(grad_bn * bn_hat, axis=0)))
     )
     bn_sums = summed(bn_parts)
     bn_shift_grad, bn_gain_grad = bn_sums[0], bn_sums[1]
@@ -324,37 +454,23 @@
     normed_parts, row_parts, gathered_sub, weight_blocks = transfer(
         5,
         ("split", "tp", normed_terms.astype(jnp.bfloat16)),
-        ("whole", "tp", row_sums),
+        ("small", "tp", row_sums),
         ("whole", "tp", quarter.reshape(-1, quarter.shape[2])),
-        ("rows", "seq", weight_parts),
+        ("reduce", "seq", weight_parts),
     )
     row_means = (summed(row_parts) / width_all).T
     normed_own = lax.dynamic_slice_in_dim(normed, tp_index * part_width, part_width, 1)
     grad_hidden = (summed(normed_parts) - row_means[:, 0:1] - normed_own * row_means[:, 1:2]) / sigma
     grad_packed = ((grad_out.astype(jnp.float32) + grad_hidden) * mask).astype(jnp.bfloat16)
-    returned, mixed_parts = transfer(
-        6,
-        ("deal", "seq", grad_packed.reshape(shards, MOST, part_width)),
-        ("split", "tp", mixed_local),
+    to_rows = (own_slots[0][:, None] == slot_ids[None, :]).astype(jnp.bfloat16)
+    grad_proj, mixed_parts = send_back(
+        6, grad_packed.reshape(shards, MOST, part_width), to_rows, mixed_local
     )
     block_out = ((hidden_part.astype(jnp.float32) + summed(mixed_parts)) * mask).astype(
         jnp.bfloat16
     )
     value_grad, gate_grad, down_grad = jnp.split(summed(weight_blocks), 3, axis=0)
-    returned = returned.reshape(shards, shards * MOST, part_width)
-    if shards <= 8:
-        to_rows = (slot_of_row[:, :, None] == slot_ids[None, None, :]).astype(jnp.bfloat16)
-        grad_proj = lax.dot_general(
-            to_rows,
-            returned,
-            (((2,), (1,)), ((0,), (0,))),
-            preferred_element_type=jnp.float32,
-        ).astype(jnp.bfloat16)
-    else:
-        grad_proj = jnp.take_along_axis(returned, slot_of_row[:, :, None], axis=1)
-    ranks = lax.axis_size("tp")
-    grad_proj = grad_proj.reshape(shards, ranks, own_rows // ranks, part_width)
-    grad_proj = jnp.swapaxes(grad_proj, 0, 1).reshape(shards * own_rows, part_width)
+    grad_proj = grad_proj.reshape(shards * own_rows, part_width)
     proj_grad = contract_rows(
         gathered_sub.reshape(shards * own_rows, gathered_sub.shape[2]), grad_proj
     )

time: 167 us -> 149 us (0.89)
  Pallas kernels: 118 us -> 103 us
  local copies, waits for them, and re-layouts: 5.61 us -> 3.66 us
    pallas_call x6 -> x5, Pallas kernels: 118 us -> 77 us  [transfer(): pl.pallas_call(functools.partial(transfer_kernel, plan), out_shape=outs,...]
    pallas_call x0 -> x1, Pallas kernels: none -> 26.5 us  [send_back(): pl.pallas_call(return_kernel, out_shape=[jax.ShapeDtypeStruct((ranks, sha...]
    dot_general x1 -> x0, matrix products: 2.65 us -> none  [body(): lax.dot_general(to_rows, returned, (((2,), (1,)), ((0,), (0,))), preferre...]
    dot_general x4, matrix products: 3.09 us -> 5.05 us  [contract_rows(): lax.dot_general(left, right, (((0,), (0,)), ((), ())), preferred_element_...]
    unnamed x48 -> x46, local copies, waits for them, and re-layouts: 4.56 us -> 2.7 us
where the time goes in v4:
time: 149 us; the launch traced here: 148 us
  Pallas kernels  103 us (69%)
  other arithmetic  21.9 us (15%)
  matrix products  17.5 us (12%)
  local copies, waits for them, and re-layouts  3.66 us (2%)
    pallas_call x5, Pallas kernels, transfer(): pl.pallas_call(functools.partial(transfer_kernel, plan), out_shape=outs,...  77 us
    pallas_call x1, Pallas kernels, send_back(): pl.pallas_call(return_kernel, out_shape=[jax.ShapeDtypeStruct((ranks, sha...  26.5 us
    dot_general x4, matrix products, contract_rows(): lax.dot_general(left, right, (((0,), (0,)), ((), ())), preferred_element_...  5.05 us
    dot_general x3, matrix products, contract_cols(): lax.dot_general(left, right, (((1,), (1,)), ((), ())), preferred_element_...  4.51 us
    reduce_sum x6, other arithmetic, summed(): return jnp.sum(parts.astype(jnp.float32), axis=0)  4.28 us
    dot_general x1, matrix products, body(): jnp.dot(to_slots, projected, preferred_element_type=jnp.float32)  3.37 us

profile of v4, /device:TPU:0, one launch (start us, length us, event | category | flops | bytes accessed | tf_op | source)
XLA Modules:
  0.0 147.6 jit_solution(2584944815289416543)
XLA Ops:
  0.7 1.0 select_reduce_fusion.1
  1.7 0.8 select_reduce_fusion.2
  2.5 0.1 select_reduce_fusion
  2.7 3.4 %convolution_convert_fusion.4 = bf16[512,256]{1,0:T(8,128)(2,1)} fusion(bf16[256,4096]{1,0:T(8,128)(2,1)} %refs_1_.1, bf16[4096,256]{1,0:T(8,128)(2,1)S(1)} %copy-done, s32[256]{0:T(256)S(1)} %bitcast.106), kind=kOutput, calls=%fused_computation.22 | convolution fusion | flops 604307456 | bytes 4457472 | tf_op jit(solution)/shard_map/dot_general | solution.py:383
  6.1 0.1 lt.68
  6.2 0.8 broadcast_select_fusion.refs_1_
  7.1 16.5 %shard_map.162 = (bf16[8,64,256]{2,1,0:T(8,128)(2,1)}, bf16[512,1024]{1,0:T(8,128)(2,1)}) custom-call(bf16[8,64,256]{2,1,0:T(8,128)(2,1)} %bitcast.79, bf16[512,256]{1,0:T(8,128)(2,1)} %broadcast_select_fusion.refs_1_), custom_call_target="tpu_custom_call" | custom-call | tf_op jit(solution)/shard_map/pallas_call | solution.py:227
  23.6 13.1 %shard_map.163 = (bf16[512,1024]{1,0:T(8,128)(2,1)}, bf16[8,64,512]{2,1,0:T(8,128)(2,1)}) custom-call(bf16[512,256]{1,0:T(8,128)(2,1)} %bitcast.73, bf16[256,4096]{1,0:T(8,128)(2,1)} %refs_1_.1), custom_call_target="tpu_custom_call" | custom-call | tf_op jit(solution)/shard_map/pallas_call | solution.py:227
  36.6 1.5 %convert_reduce_fusion = f32[512]{0:T(512)S(1)} fusion(bf16[512,1024]{1,0:T(8,128)(2,1)} %get-tuple-element.18), kind=kLoop, calls=%fused_computation.1 | loop fusion | flops 1048064 | bytes 1050624 | tf_op jit(solution)/shard_map/reduce_sum | solution.py:401
  38.2 1.6 %fusion.2 = f32[512]{0:T(512)S(1)} fusion(bf16[512,1024]{1,0:T(8,128)(2,1)} %get-tuple-element.18, f32[512]{0:T(512)S(1)} %broadcast_multiply_fusion.1), kind=kLoop, calls=%fused_computation.4 | loop fusion | flops 2096640 | bytes 1052672 | tf_op jit(solution)/shard_map/reduce_sum | solution.py:402
  39.8 1.7 %fusion.52 = (bf16[512,1024]{1,0:T(8,128)(2,1)S(1)}, f32[512,1024]{1,0:T(8,128)}) fusion(f32[512]{0:T(512)S(1)} %add_sqrt_fusion, f32[512]{0:T(512)S(1)} %broadcast_multiply_fusion.1, bf16[512,1024]{1,0:T(8,128)(2,1)S(1)} %copy-done.2), kind=kLoop, calls=%fused_computation.116 | loop fusion | flops 2097152 | bytes 4198400 | tf_op jit(solution)/shard_map/convert_element_type | solution.py:404
  41.5 0.5 fusion.6
  42.0 0.9 copy-done.6
  42.9 1.2 multiply_multiply_fusion.1
  44.2 0.7 multiply_reduce_fusion.3
  44.9 0.7 maximum_maximum_fusion.1.refs_0_
  45.6 8.4 %shard_map.164 = f32[8,8,256]{2,1,0:T(8,128)} custom-call(f32[8,256]{1,0:T(8,128)} %maximum_maximum_fusion.1.refs_0_), custom_call_target="tpu_custom_call" | custom-call | tf_op jit(solution)/shard_map/pallas_call | solution.py:227
  54.1 0.9 reduce_sum.160
  55.0 2.9 %fusion.48 = (f32[256]{0:T(256)S(1)}, f32[256]{0:T(256)S(1)}, f32[512,256]{1,0:T(8,128)}) fusion(f32[512,256]{1,0:T(8,128)S(1)} %fusion.40, f32[512]{0:T(512)S(1)} %convert_element_type.81, f32[256]{0:T(256)S(1)} %copy-done.22, f32[256]{0:T(256)S(1)} %copy-done.20, bf16[512,1024]{1,0:T(8,128)(2,1)} %get-tuple-element.19, bf16[1024,256]{1,0:T(8,128)(2,1)} %param.18), kind=kOutput, calls=%fused_computation.114 | convolution fusion | flops 270269952 | bytes 2627584 | tf_op jit(solution)/shard_map/dot_general | solution.py:424
  57.9 0.7 maximum_maximum_fusion.2.refs_0_
  58.6 7.3 %shard_map.165 = f32[8,8,256]{2,1,0:T(8,128)} custom-call(f32[8,256]{1,0:T(8,128)} %maximum_maximum_fusion.2.refs_0_), custom_call_target="tpu_custom_call" | custom-call | tf_op jit(solution)/shard_map/pallas_call | solution.py:227
  65.9 0.9 reduce_sum.163
  66.8 1.3 multiply_multiply_fusion
  68.1 0.5 fusion.32
  68.6 0.2 multiply_convert_fusion.3
  68.9 0.5 convolution_convert_fusion.3
  69.4 0.5 convolution_convert_fusion.2
  69.9 0.3 copy-done.21
  70.3 0.6 convolution_convert_fusion.1
  70.9 1.3 pad_maximum_fusion.refs_3_
  72.2 0.5 fusion.58
  72.6 1.1 copy-done.1
  73.7 0.1 copy-done.13
  73.8 1.5 %fusion.47 = (f32[512]{0:T(512)S(1)}, f32[512]{0:T(512)S(1)}, bf16[512,1024]{1,0:T(8,128)(2,1)}) fusion(f32[512,1024]{1,0:T(8,128)S(1)} %copy-done.1, f32[512,1024]{1,0:T(8,128)S(1)} %fusion.58, bf16[512,256]{1,0:T(8,128)(2,1)S(1)} %get-tuple-element.39, bf16[1024,256]{1,0:T(8,128)(2,1)S(1)} %copy-done.13), kind=kOutput, calls=%fused_computation.113 | convolution fusion | flops 271055872 | bytes 6033408 | tf_op jit(solution)/shard_map/dot_general | solution.py:343
  75.4 0.7 maximum_maximum_fusion.refs_1_
  76.0 31.6 %shard_map.166 = (bf16[4,512,256]{2,1,0:T(8,128)(2,1)}, f32[4,8,512]{2,1,0:T(8,128)}, bf16[4,512,512]{2,1,0:T(8,128)(2,1)}, bf16[4,384,256]{2,1,0:T(8,128)(2,1)}) custom-call(bf16[512,1024]{1,0:T(8,128)(2,1)} %get-tuple-element.38.refs_0_, f32[8,512]{1,0:T(8,128)} %maximum_maximum_fusion.refs_1_, bf16[512,512]{1,0:T(8,128)(2,1)} %bitcast.75, ...), custom_call_target="tpu_custom_call" | custom-call | tf_op jit(solution)/shard_map/pallas_call | solution.py:227
  107.7 1.5 convert_reduce_fusion.2
  109.2 0.9 reduce_sum.167
  110.1 2.2 %multiply_convert_fusion.1 = bf16[512,256]{1,0:T(8,128)(2,1)} fusion(f32[512,1024]{1,0:T(8,128)} %get-tuple-element.37, s32[]{:T(128)S(6)} %select_n.27, f32[512,256]{1,0:T(8,128)S(1)} %convert_reduce_fusion.2, f32[512]{0:T(512)S(1)} %add_sqrt_fusion, f32[512]{0:T(512)S(1)} %bitcast.105, f32[512]{0:T(512)S(1)} %bitcast.104, f32[512]{0:T(512)S(1)} %convert_element_type.81, ...), kind=kLoop, calls=%fused_computation.77 | loop fusion | flops 1179648 | bytes 1581572 | tf_op jit(solution)/shard_map/convert_element_type | solution.py:464
  112.2 2.5 %convolution_convert_fusion.mixed = bf16[512,1024]{1,0:T(8,128)(2,1)} fusion(bf16[1024,256]{1,0:T(8,128)(2,1)} %param.18, f32[512,256]{1,0:T(8,128)S(1)} %copy-done.16, f32[256]{0:T(256)S(1)} %copy-done.22, f32[256]{0:T(256)S(1)} %copy-done.20), kind=kOutput, calls=%fused_computation.11 | convolution fusion | flops 269877248 | bytes 2099200 | tf_op jit(solution)/shard_map/dot_general | solution.py:343
  114.7 0.8 fusion.41.to_rows
  115.5 26.5 %shard_map.167 = (bf16[4,8,64,256]{3,2,1,0:T(8,128)(2,1)}, bf16[4,512,256]{2,1,0:T(8,128)(2,1)}) custom-call(bf16[8,64,256]{2,1,0:T(8,128)(2,1)} %bitcast.74, bf16[256,512]{1,0:T(8,128)(2,1)} %fusion.41.to_rows, bf16[512,1024]{1,0:T(8,128)(2,1)} %convolution_convert_fusion.mixed), custom_call_target="tpu_custom_call" | custom-call | tf_op jit(solution)/shard_map/pallas_call | solution.py:279
  142.1 3.5 %fusion.59 = f32[512,256]{1,0:T(8,128)} fusion(bf16[2048,512]{1,0:T(8,128)(2,1)} %bitcast.69, bf16[2048,256]{1,0:T(8,128)(2,1)} %bitcast.72), kind=kOutput, calls=%fused_computation.122 | convolution fusion | flops 536870912 | bytes 3670016 | tf_op jit(solution)/shard_map/dot_general | solution.py:337
  145.6 0.1 convert_reduce_fusion.1
  145.7 0.8 multiply_convert_fusion
  146.6 0.1 copy-done.11
  146.7 0.1 convert_reduce_fusion.3
  146.8 0.8 fusion.54
  (57 shorter events, 0.4 us)
Async XLA Ops:
  0.6 2.0 %copy-start = (bf16[4096,256]{1,0:T(8,128)(2,1)S(1)}, bf16[4096,256]{1,0:T(8,128)(2,1)}, u32[]{:S(2)}) copy-start(bf16[4096,256]{1,0:T(8,128)(2,1)} %param.12) | copy-start | bytes 6291460
  2.7 3.5 %copy-start.10 = (bf16[512,256]{1,0:T(8,128)(2,1)S(1)}, bf16[512,256]{1,0:T(8,128)(2,1)}, u32[]{:S(2)}) copy-start(bf16[512,256]{1,0:T(8,128)(2,1)} %param.21) | copy-start | bytes 786436
  36.6 3.2 %copy-start.2 = (bf16[512,1024]{1,0:T(8,128)(2,1)S(1)}, bf16[512,1024]{1,0:T(8,128)(2,1)}, u32[]{:S(2)}) copy-start(bf16[512,1024]{1,0:T(8,128)(2,1)} %get-tuple-element.18) | copy-start | bytes 3145732
  39.8 1.7 %copy-start.12 = (bf16[1024,256]{1,0:T(8,128)(2,1)S(1)}, bf16[1024,256]{1,0:T(8,128)(2,1)}, u32[]{:S(2)}) copy-start(bf16[1024,256]{1,0:T(8,128)(2,1)} %param.14) | copy-start | bytes 1572868
  41.5 2.6 %copy-start.3 = (bf16[512,1024]{1,0:T(8,128)(2,1)}, bf16[512,1024]{1,0:T(8,128)(2,1)S(1)}, u32[]{:S(2)}) copy-start(bf16[512,1024]{1,0:T(8,128)(2,1)S(1)} %get-tuple-element.36) | copy-start | bytes 3145732
  41.5 1.4 copy-start.6
  42.0 2.2 %copy-start.17 = (f32[9,256]{1,0:T(8,128)S(1)}, f32[9,256]{1,0:T(8,128)}, u32[]{:S(2)}) copy-start(f32[9,256]{1,0:T(8,128)} %param.15) | copy-start | bytes 27652
  42.9 12.1 %copy-start.20 = (f32[256]{0:T(256)S(1)}, f32[256]{0:T(256)}, u32[]{:S(2)}) copy-start(f32[256]{0:T(256)} %param.16) | copy-start | bytes 3076
  42.9 12.1 %copy-start.22 = (f32[256]{0:T(256)S(1)}, f32[256]{0:T(256)}, u32[]{:S(2)}) copy-start(f32[256]{0:T(256)} %param.17) | copy-start | bytes 3076
  55.0 2.9 %copy-start.14 = (f32[512,256]{1,0:T(8,128)}, f32[512,256]{1,0:T(8,128)S(1)}, u32[]{:S(2)}) copy-start(f32[512,256]{1,0:T(8,128)S(1)} %fusion.40) | copy-start | bytes 1572868
  66.7 1.9 %copy-start.5 = (f32[512,256]{1,0:T(8,128)S(1)}, f32[512,256]{1,0:T(8,128)}, u32[]{:S(2)}) copy-start(f32[512,256]{1,0:T(8,128)} %get-tuple-element.64) | copy-start | bytes 1572868
  66.7 2.1 %copy-start.18 = (f32[1,256]{1,0:T(1,128)}, f32[1,256]{1,0:T(1,128)S(1)}, u32[]{:S(2)}) copy-start(f32[1,256]{1,0:T(1,128)S(1)} %get-tuple-element.55) | copy-start | bytes 3076
  66.7 2.1 %copy-start.19 = (f32[1,256]{1,0:T(1,128)}, f32[1,256]{1,0:T(1,128)S(1)}, u32[]{:S(2)}) copy-start(f32[1,256]{1,0:T(1,128)S(1)} %get-tuple-element.56) | copy-start | bytes 3076
  66.8 2.1 %copy-start.4 = (bf16[512,1024]{1,0:T(8,128)(2,1)S(1)}, bf16[512,1024]{1,0:T(8,128)(2,1)}, u32[]{:S(2)}) copy-start(bf16[512,1024]{1,0:T(8,128)(2,1)} %copy-done.3) | copy-start | bytes 3145732
  68.9 1.0 copy-start.15
  68.9 1.4 copy-start.21
  70.9 1.3 copy-start.7
  72.1 1.6 %copy-start.1 = (f32[512,1024]{1,0:T(8,128)S(1)}, f32[512,1024]{1,0:T(8,128)}, u32[]{:S(2)}) copy-start(f32[512,1024]{1,0:T(8,128)} %get-tuple-element.37) | copy-start | bytes 6291460
  72.2 1.7 %copy-start.13 = (bf16[1024,256]{1,0:T(8,128)(2,1)S(1)}, bf16[1024,256]{1,0:T(8,128)(2,1)}, u32[]{:S(2)}) copy-start(bf16[1024,256]{1,0:T(8,128)(2,1)} %param.14) | copy-start | bytes 1572868
  107.7 4.5 %copy-start.16 = (f32[512,256]{1,0:T(8,128)S(1)}, f32[512,256]{1,0:T(8,128)}, u32[]{:S(2)}) copy-start(f32[512,256]{1,0:T(8,128)} %copy-done.14) | copy-start | bytes 1572868
  142.0 3.5 %copy-start.8 = (bf16[4,512,256]{2,1,0:T(8,128)(2,1)S(1)}, bf16[4,512,256]{2,1,0:T(8,128)(2,1)}, u32[]{:S(2)}) copy-start(bf16[4,512,256]{2,1,0:T(8,128)(2,1)} %get-tuple-element.23) | copy-start | bytes 3145732
  142.1 3.7 %copy-start.9 = (bf16[8,64,256]{2,1,0:T(8,128)(2,1)S(1)}, bf16[8,64,256]{2,1,0:T(8,128)(2,1)}, u32[]{:S(2)}) copy-start(bf16[8,64,256]{2,1,0:T(8,128)(2,1)} %get-tuple-element.17) | copy-start | bytes 786436
  145.6 1.1 copy-start.11

commit v5 on v4

--- a/solution.py
+++ b/solution.py
@@ -138,6 +138,13 @@
     return copies
 
 
+def share_of(source, axis, index):
+    if len(source.shape) == 3:
+        return source.at[index]
+    width = source.shape[1] // lax.axis_size(axis)
+    return source.at[:, pl.ds(pl.multiple_of(index * width, 128), width)]
+
+
 def start_reduce(axis, source, landing, send, recv):
     half = lax.axis_size(axis) // 2
     me = lax.axis_index(axis)
@@ -145,7 +152,7 @@
     copies = []
     for step in range(half):
         line = lax.rem(me // 2 + 1 + step, half)
-        block = source.at[2 * line + lax.rem(partner, 2)]
+        block = share_of(source, axis, 2 * line + lax.rem(partner, 2))
         copies.append(
             push(block, landing.at[step], send.at[step], recv.at[step], axis, partner)
         )
@@ -160,7 +167,8 @@
         line = lax.rem(me // 2 + 1 + step, half)
         peer = 2 * line + lax.rem(me, 2)
         firsts[step].wait()
-        both = source[peer].astype(jnp.float32) + landing[step].astype(jnp.float32)
+        mine = share_of(source, axis, peer)[...]
+        both = mine.astype(jnp.float32) + landing[step].astype(jnp.float32)
         partial[step] = both.astype(partial.dtype)
         place = target.at[me // 2]
         if step < half - 1:
@@ -182,21 +190,22 @@
     local_sem = refs[4 * count]
     rooms = refs[4 * count + 1 :]
     greet(sorted({axis for _, axis in plan}))
-    copies, relays, firsts, reduced = [], [], [], None
+    copies, relays, reduced = [], [], []
     for which, (kind, axis) in enumerate(plan):
         source, target = sources[which], targets[which]
         send, recv, local = sends[which], recvs[which], local_sem.at[which]
         if kind == "reduce":
-            firsts = start_reduce(axis, source, rooms[0], send, recv)
-            reduced = (axis, firsts, source, rooms[0], rooms[1], target, send, recv, local)
+            landing, partial = rooms[2 * len(reduced)], rooms[2 * len(reduced) + 1]
+            firsts = start_reduce(axis, source, landing, send, recv)
+            reduced.append((axis, firsts, source, landing, partial, target, send, recv, local))
         elif kind in GATHERS:
             started, waiting = start_gather(kind, axis, source, target, send, recv, local)
             copies += started
             relays += waiting
         else:
             copies += start_direct(kind, axis, source, target, send, recv, local)
-    if reduced is not None:
-        copies += finish_reduce(*reduced)
+    for state in reduced:
+        copies += finish_reduce(*state)
     copies += relay_all(relays)
     for copy in copies:
         copy.wait()
@@ -216,8 +225,11 @@
         elif kind == "quarter":
             shape = (size, shape[0] // lax.axis_size("tp"), shape[1] // size)
         elif kind == "reduce":
-            shape = (size // 2,) + shape[1:]
-            rooms = [pltpu.VMEM(shape, array.dtype)] * 2
+            if len(shape) == 2:
+                shape = (size // 2, shape[0], shape[1] // size)
+            else:
+                shape = (size // 2,) + shape[1:]
+            rooms += [pltpu.VMEM(shape, array.dtype)] * 2
         elif kind in ("whole", "small"):
             shape = (size,) + shape
         outs.append(jax.ShapeDtypeStruct(shape, array.dtype))
@@ -238,8 +250,10 @@
     packed,
     to_rows,
     mixed,
+    quarter,
     gathered,
     mixed_parts,
+    sub,
     landing,
     owned,
     packed_send,
@@ -248,6 +262,8 @@
     mixed_recv,
     owned_send,
     owned_recv,
+    sub_send,
+    sub_recv,
     local_sem,
 ):
     greet(("seq", "tp"))
@@ -255,6 +271,10 @@
         "rows", "seq", packed, landing, packed_send, packed_recv, local_sem.at[0]
     )
     copies = start_direct("split", "tp", mixed, mixed_parts, mixed_send, mixed_recv, local_sem.at[1])
+    sub_copies, sub_relays = start_gather(
+        "whole", "tp", quarter, sub, sub_send, sub_recv, local_sem.at[3]
+    )
+    copies += sub_copies
     for copy in arrivals:
         copy.wait()
     frames = landing[...].reshape(-1, landing.shape[2])
@@ -264,12 +284,12 @@
         "deal", "seq", owned, gathered, owned_send, owned_recv, local_sem.at[2]
     )
     copies += started
-    copies += relay_all(relays)
+    copies += relay_all(relays + sub_relays)
     for copy in copies:
         copy.wait()
 
 
-def send_back(number, packed, to_rows, mixed):
+def send_back(number, packed, to_rows, mixed, quarter):
     shards = lax.axis_size("seq")
     ranks = lax.axis_size("tp")
     height = to_rows.shape[0] // ranks
@@ -281,13 +301,15 @@
         out_shape=[
             jax.ShapeDtypeStruct((ranks, shards, height, width), packed.dtype),
             jax.ShapeDtypeStruct((ranks, mixed.shape[0], mixed.shape[1] // ranks), mixed.dtype),
+            jax.ShapeDtypeStruct((ranks,) + quarter.shape, quarter.dtype),
         ],
         in_specs=[
             pl.BlockSpec(memory_space=pl.ANY),
             pl.BlockSpec(memory_space=pltpu.VMEM),
             pl.BlockSpec(memory_space=pl.ANY),
+            pl.BlockSpec(memory_space=pl.ANY),
         ],
-        out_specs=[pl.BlockSpec(memory_space=pl.ANY)] * 2,
+        out_specs=[pl.BlockSpec(memory_space=pl.ANY)] * 3,
         scratch_shapes=[
             pltpu.VMEM(packed.shape, packed.dtype),
             pltpu.VMEM(owned, packed.dtype),
@@ -297,10 +319,111 @@
             dma((ranks,)),
             dma((shards * PIECES,)),
             dma((shards * PIECES,)),
+            dma((ranks * PIECES,)),
+            dma((ranks * PIECES,)),
+            dma((4,)),
+        ],
+        compiler_params=pltpu.CompilerParams(collective_id=number, has_side_effects=True),
+    )(packed, to_rows, mixed, quarter)
+
+
+def spread_kernel(
+    outgoing,
+    grad_out,
+    subsampled,
+    arrived,
+    hidden,
+    grad_full,
+    quarter,
+    out_send,
+    out_recv,
+    hidden_send,
+    hidden_recv,
+    grad_send,
+    grad_recv,
+    quarter_send,
+    quarter_recv,
+    block_sem,
+    local_sem,
+):
+    greet(("seq", "tp"))
+    shards, ranks = lax.axis_size("seq"), lax.axis_size("tp")
+    me, rank = lax.axis_index("seq"), lax.axis_index("tp")
+    height, width = outgoing.shape[1], outgoing.shape[2]
+    arrivals = start_direct(
+        "rows", "seq", outgoing, arrived, out_send, out_recv, local_sem.at[0]
+    )
+    copies, grad_relays = start_gather(
+        "columns", "tp", grad_out, grad_full, grad_send, grad_recv, local_sem.at[1]
+    )
+    copies += start_direct(
+        "quarter", "seq", subsampled, quarter, quarter_send, quarter_recv, local_sem.at[2]
+    )
+
+    def place_of(owner, column):
+        rows = pl.ds(pl.multiple_of(owner * height, 16), height)
+        return hidden.at[rows, pl.ds(pl.multiple_of(column * width, 128), width)]
+
+    arrivals = arrivals[-1:] + arrivals[:-1]
+    firsts = []
+    for step in range(shards):
+        owner = lax.rem(me + shards - step, shards)
+        arrivals[step].wait()
+        block, place = arrived.at[owner], place_of(owner, rank)
+        for hop in range(1, ranks // 2):
+            slot = hop * shards + step
+            peer = lax.rem(rank + 2 * hop, ranks)
+            first = push(block, place, hidden_send.at[slot], hidden_recv.at[slot], "tp", peer)
+            firsts.append((first, owner, hop, step))
+        copies.append(
+            push(block, place, hidden_send.at[step], hidden_recv.at[step], "tp", partner_of(rank))
+        )
+        own = pltpu.make_async_copy(block, place, block_sem.at[step])
+        own.start()
+        copies.append(own)
+    copies += relay_all(grad_relays)
+    for first, owner, hop, step in firsts:
+        first.wait()
+        place = place_of(owner, lax.rem(rank + ranks - 2 * hop, ranks))
+        slot = (ranks // 2 + hop - 1) * shards + step
+        copies.append(
+            push(
+                place, place, hidden_send.at[slot], hidden_recv.at[slot], "tp", partner_of(rank)
+            )
+        )
+    for copy in copies:
+        copy.wait()
+
+
+def spread(number, outgoing, grad_out, subsampled):
+    shards, ranks = lax.axis_size("seq"), lax.axis_size("tp")
+    full = (grad_out.shape[0], grad_out.shape[1] * ranks)
+    quarter = (shards, subsampled.shape[0] // ranks, subsampled.shape[1] // shards)
+    dma = pltpu.SemaphoreType.DMA
+    return pl.pallas_call(
+        spread_kernel,
+        out_shape=[
+            jax.ShapeDtypeStruct(outgoing.shape, outgoing.dtype),
+            jax.ShapeDtypeStruct(full, outgoing.dtype),
+            jax.ShapeDtypeStruct(full, grad_out.dtype),
+            jax.ShapeDtypeStruct(quarter, subsampled.dtype),
+        ],
+        in_specs=[pl.BlockSpec(memory_space=pl.ANY)] * 3,
+        out_specs=[pl.BlockSpec(memory_space=pl.ANY)] * 4,
+        scratch_shapes=[
+            dma((shards,)),
+            dma((shards,)),
+            dma((ranks * shards,)),
+            dma((ranks * shards,)),
+            dma((ranks * PIECES,)),
+            dma((ranks * PIECES,)),
+            dma((shards,)),
+            dma((shards,)),
+            dma((shards,)),
             dma((3,)),
         ],
         compiler_params=pltpu.CompilerParams(collective_id=number, has_side_effects=True),
-    )(packed, to_rows, mixed)
+    )(outgoing, grad_out, subsampled)
 
 
 def summed(parts):
@@ -388,15 +511,10 @@
     valid = (frame_pos[None, :] < in_lengths[:, None]).reshape(-1, 1)
     mask = valid.astype(jnp.float32)
     grad_out = jnp.where(valid, out_grad, jnp.zeros((), jnp.bfloat16))
-    arrived, grad_full = transfer(
-        1,
-        ("rows", "seq", outgoing.reshape(shards, MOST, part_width)),
-        ("columns", "tp", grad_out),
+    arrived, hidden_full, grad_full, quarter = spread(
+        1, outgoing.reshape(shards, MOST, part_width), grad_out, subsampled
     )
     hidden_part = arrived.reshape(shards * MOST, part_width)
-    hidden_full, quarter = transfer(
-        2, ("columns", "tp", hidden_part), ("quarter", "seq", subsampled)
-    )
     hidden32 = hidden_full.astype(jnp.float32)
     centred = hidden32 - jnp.mean(hidden32, axis=1, keepdims=True)
     sigma = jnp.sqrt(jnp.mean(centred * centred, axis=1, keepdims=True) + 1e-05)
@@ -451,11 +569,10 @@
         ],
         axis=1,
     )
-    normed_parts, row_parts, gathered_sub, weight_blocks = transfer(
+    normed_parts, row_parts, weight_blocks = transfer(
         5,
-        ("split", "tp", normed_terms.astype(jnp.bfloat16)),
+        ("reduce", "tp", normed_terms.astype(jnp.bfloat16)),
         ("small", "tp", row_sums),
-        ("whole", "tp", quarter.reshape(-1, quarter.shape[2])),
         ("reduce", "seq", weight_parts),
     )
     row_means = (summed(row_parts) / width_all).T
@@ -463,8 +580,12 @@
     grad_hidden = (summed(normed_parts) - row_means[:, 0:1] - normed_own * row_means[:, 1:2]) / sigma
     grad_packed = ((grad_out.astype(jnp.float32) + grad_hidden) * mask).astype(jnp.bfloat16)
     to_rows = (own_slots[0][:, None] == slot_ids[None, :]).astype(jnp.bfloat16)
-    grad_proj, mixed_parts = send_back(
-        6, grad_packed.reshape(shards, MOST, part_width), to_rows, mixed_local
+    grad_proj, mixed_parts, gathered_sub = send_back(
+        6,
+        grad_packed.reshape(shards, MOST, part_width),
+        to_rows,
+        mixed_local,
+        quarter.reshape(-1, quarter.shape[2]),
     )
     block_out = ((hidden_part.astype(jnp.float32) + summed(mixed_parts)) * mask).astype(
         jnp.bfloat16

time: 149 us -> 144 us (0.966)
  Pallas kernels: 103 us -> 99 us
    pallas_call x5 -> x3, Pallas kernels: 77 us -> 40.4 us  [transfer(): pl.pallas_call(functools.partial(transfer_kernel, plan), out_shape=outs,...]
    pallas_call x0 -> x1, Pallas kernels: none -> 27.2 us  [spread(): pl.pallas_call(spread_kernel, out_shape=[jax.ShapeDtypeStruct(outgoing.sh...]
    pallas_call x1, Pallas kernels: 26.5 us -> 31.4 us  [send_back(): pl.pallas_call(return_kernel, out_shape=[jax.ShapeDtypeStruct((ranks, sha...]
where the time goes in v5:
time: 144 us; the launch traced here: 143 us
  Pallas kernels  99 us (69%)
  other arithmetic  21.6 us (15%)
  matrix products  17.5 us (12%)
  local copies, waits for them, and re-layouts  3.68 us (3%)
    pallas_call x3, Pallas kernels, transfer(): pl.pallas_call(functools.partial(transfer_kernel, plan), out_shape=outs,...  40.4 us
    pallas_call x1, Pallas kernels, send_back(): pl.pallas_call(return_kernel, out_shape=[jax.ShapeDtypeStruct((ranks, sha...  31.4 us
    pallas_call x1, Pallas kernels, spread(): pl.pallas_call(spread_kernel, out_shape=[jax.ShapeDtypeStruct(outgoing.sh...  27.2 us
    dot_general x4, matrix products, contract_rows(): lax.dot_general(left, right, (((0,), (0,)), ((), ())), preferred_element_...  5.05 us
    dot_general x3, matrix products, contract_cols(): lax.dot_general(left, right, (((1,), (1,)), ((), ())), preferred_element_...  4.49 us
    reduce_sum x6, other arithmetic, summed(): return jnp.sum(parts.astype(jnp.float32), axis=0)  3.97 us
    dot_general x1, matrix products, body(): jnp.dot(to_slots, projected, preferred_element_type=jnp.float32)  3.37 us
    dot_general x1, matrix products, body(): jnp.dot(grad_full, down_weight, preferred_element_type=jnp.float32)  2.89 us

profile of v5, /device:TPU:0, one launch (start us, length us, event | category | flops | bytes accessed | tf_op | source)
XLA Modules:
  0.0 142.8 jit_solution(13217913949620286469)
XLA Ops:
  0.7 1.0 select_reduce_fusion.1
  1.7 0.8 select_reduce_fusion.2
  2.5 0.1 select_reduce_fusion
  2.7 3.4 %convolution_convert_fusion.4 = bf16[512,256]{1,0:T(8,128)(2,1)} fusion(bf16[256,4096]{1,0:T(8,128)(2,1)} %subsampled.1, bf16[4096,256]{1,0:T(8,128)(2,1)S(1)} %copy-done, s32[256]{0:T(256)S(1)} %bitcast.106), kind=kOutput, calls=%fused_computation.21 | convolution fusion | flops 604307456 | bytes 4457472 | tf_op jit(solution)/shard_map/dot_general | solution.py:506
  6.1 0.1 lt.68
  6.2 0.8 broadcast_select_fusion.grad_out
  7.1 27.2 %shard_map.162 = (bf16[8,64,256]{2,1,0:T(8,128)(2,1)}, bf16[512,1024]{1,0:T(8,128)(2,1)}, bf16[512,1024]{1,0:T(8,128)(2,1)}, bf16[8,64,512]{2,1,0:T(8,128)(2,1)}) custom-call(bf16[8,64,256]{2,1,0:T(8,128)(2,1)} %bitcast.79, bf16[512,256]{1,0:T(8,128)(2,1)} %broadcast_select_fusion.grad_out, bf16[256,4096]{1,0:T(8,128)(2,1)} %subsampled.1), custom_call_target="tpu_custom_call" | custom-call | tf_op jit(solution)/shard_map/pallas_call | solution.py:403
  34.3 1.5 %convert_reduce_fusion = f32[512]{0:T(512)S(1)} fusion(bf16[512,1024]{1,0:T(8,128)(2,1)} %get-tuple-element.18), kind=kLoop, calls=%fused_computation.1 | loop fusion | flops 1048064 | bytes 1050624 | tf_op jit(solution)/shard_map/reduce_sum | solution.py:519
  35.9 1.6 %fusion.2 = f32[512]{0:T(512)S(1)} fusion(bf16[512,1024]{1,0:T(8,128)(2,1)} %get-tuple-element.18, f32[512]{0:T(512)S(1)} %broadcast_multiply_fusion.1), kind=kLoop, calls=%fused_computation.4 | loop fusion | flops 2096640 | bytes 1052672 | tf_op jit(solution)/shard_map/reduce_sum | solution.py:520
  37.5 1.7 %fusion.54 = (bf16[512,1024]{1,0:T(8,128)(2,1)S(1)}, f32[512,1024]{1,0:T(8,128)}) fusion(f32[512]{0:T(512)S(1)} %add_sqrt_fusion, f32[512]{0:T(512)S(1)} %broadcast_multiply_fusion.1, bf16[512,1024]{1,0:T(8,128)(2,1)S(1)} %copy-done.2), kind=kLoop, calls=%fused_computation.118 | loop fusion | flops 2097152 | bytes 4198400 | tf_op jit(solution)/shard_map/convert_element_type | solution.py:522
  39.2 0.5 fusion.6
  39.7 0.9 copy-done.6
  40.6 1.2 multiply_multiply_fusion.1
  41.9 0.7 multiply_reduce_fusion.3
  42.5 0.1 pad.20.clone
  42.6 0.7 maximum_maximum_fusion.1.refs_0_
  43.3 6.8 %shard_map.163 = f32[8,8,256]{2,1,0:T(8,128)} custom-call(f32[8,256]{1,0:T(8,128)} %maximum_maximum_fusion.1.refs_0_), custom_call_target="tpu_custom_call" | custom-call | tf_op jit(solution)/shard_map/pallas_call | solution.py:239
  50.1 0.9 reduce_sum.160
  51.1 2.9 %fusion.50 = (f32[256]{0:T(256)S(1)}, f32[256]{0:T(256)S(1)}, f32[512,256]{1,0:T(8,128)}) fusion(f32[512,256]{1,0:T(8,128)S(1)} %fusion.42, f32[512]{0:T(512)S(1)} %convert_element_type.85, f32[256]{0:T(256)S(1)} %copy-done.21, f32[256]{0:T(256)S(1)} %copy-done.19, bf16[512,1024]{1,0:T(8,128)(2,1)} %get-tuple-element.19, bf16[1024,256]{1,0:T(8,128)(2,1)} %param.18), kind=kOutput, calls=%fused_computation.116 | convolution fusion | flops 270269952 | bytes 2627584 | tf_op jit(solution)/shard_map/dot_general | solution.py:542
  54.0 0.7 maximum_maximum_fusion.2.refs_0_
  54.6 6.8 %shard_map.164 = f32[8,8,256]{2,1,0:T(8,128)} custom-call(f32[8,256]{1,0:T(8,128)} %maximum_maximum_fusion.2.refs_0_), custom_call_target="tpu_custom_call" | custom-call | tf_op jit(solution)/shard_map/pallas_call | solution.py:239
  61.5 0.9 reduce_sum.163
  62.4 1.3 multiply_multiply_fusion
  63.7 0.5 fusion.32
  64.3 0.2 multiply_convert_fusion.2
  64.5 0.5 convolution_convert_fusion.3
  65.0 0.5 convolution_convert_fusion.2
  65.6 0.3 copy-done.20
  65.9 0.6 convolution_convert_fusion.1
  66.5 1.3 pad_maximum_fusion.refs_2_
  67.8 0.5 fusion.60
  68.2 1.1 copy-done.1
  69.4 0.1 copy-done.12
  69.4 1.5 %fusion.49 = (f32[512]{0:T(512)S(1)}, f32[512]{0:T(512)S(1)}, bf16[512,1024]{1,0:T(8,128)(2,1)}) fusion(f32[512,1024]{1,0:T(8,128)S(1)} %copy-done.1, f32[512,1024]{1,0:T(8,128)S(1)} %fusion.60, bf16[512,256]{1,0:T(8,128)(2,1)S(1)} %get-tuple-element.39, bf16[1024,256]{1,0:T(8,128)(2,1)S(1)} %copy-done.12), kind=kOutput, calls=%fused_computation.115 | convolution fusion | flops 271055872 | bytes 6033408 | tf_op jit(solution)/shard_map/dot_general | solution.py:466
  71.0 0.7 maximum_maximum_fusion.refs_1_
  71.6 26.7 %shard_map.165 = (bf16[2,512,256]{2,1,0:T(8,128)(2,1)}, f32[4,8,512]{2,1,0:T(8,128)}, bf16[4,384,256]{2,1,0:T(8,128)(2,1)}) custom-call(bf16[512,1024]{1,0:T(8,128)(2,1)} %get-tuple-element.38.refs_0_, f32[8,512]{1,0:T(8,128)} %maximum_maximum_fusion.refs_1_, bf16[8,384,256]{2,1,0:T(8,128)(2,1)} %pad_maximum_fusion.refs_2_), custom_call_target="tpu_custom_call" | custom-call | tf_op jit(solution)/shard_map/pallas_call | solution.py:239
  98.3 1.2 convert_reduce_fusion.3
  99.5 0.9 reduce_sum.167
  100.4 2.2 %multiply_convert_fusion = bf16[512,256]{1,0:T(8,128)(2,1)} fusion(f32[512,1024]{1,0:T(8,128)} %get-tuple-element.37, s32[]{:T(128)S(6)} %select_n.27, f32[512,256]{1,0:T(8,128)S(1)} %convert_reduce_fusion.3, f32[512]{0:T(512)S(1)} %add_sqrt_fusion, f32[512]{0:T(512)S(1)} %bitcast.105, f32[512]{0:T(512)S(1)} %bitcast.104, f32[512]{0:T(512)S(1)} %convert_element_type.85, ...), kind=kLoop, calls=%fused_computation.79 | loop fusion | flops 1179648 | bytes 1581572 | tf_op jit(solution)/shard_map/convert_element_type | solution.py:581
  102.5 2.5 %convolution_convert_fusion.mixed = bf16[512,1024]{1,0:T(8,128)(2,1)} fusion(bf16[1024,256]{1,0:T(8,128)(2,1)} %param.18, f32[512,256]{1,0:T(8,128)S(1)} %copy-done.14, f32[256]{0:T(256)S(1)} %copy-done.21, f32[256]{0:T(256)S(1)} %copy-done.19), kind=kOutput, calls=%fused_computation.10 | convolution fusion | flops 269877248 | bytes 2099200 | tf_op jit(solution)/shard_map/dot_general | solution.py:466
  105.1 0.8 fusion.43.to_rows
  105.9 31.4 %shard_map.166 = (bf16[4,8,64,256]{3,2,1,0:T(8,128)(2,1)}, bf16[4,512,256]{2,1,0:T(8,128)(2,1)}, bf16[4,512,512]{2,1,0:T(8,128)(2,1)}) custom-call(bf16[8,64,256]{2,1,0:T(8,128)(2,1)} %bitcast.74, bf16[256,512]{1,0:T(8,128)(2,1)} %fusion.43.to_rows, bf16[512,1024]{1,0:T(8,128)(2,1)} %convolution_convert_fusion.mixed, bf16[512,512]{1,0:T(8,128)(2,1)} %bitcast.75), custom_call_target="tpu_custom_call" | custom-call | tf_op jit(solution)/shard_map/pallas_call | solution.py:299
  137.3 3.5 %fusion.61 = f32[512,256]{1,0:T(8,128)} fusion(bf16[2048,512]{1,0:T(8,128)(2,1)} %bitcast.70, bf16[2048,256]{1,0:T(8,128)(2,1)} %bitcast.73), kind=kOutput, calls=%fused_computation.124 | convolution fusion | flops 536870912 | bytes 3670016 | tf_op jit(solution)/shard_map/dot_general | solution.py:460
  140.8 0.1 convert_reduce_fusion.1
  140.9 0.8 fusion.41
  141.8 0.1 copy-done.10
  141.9 0.1 convert_reduce_fusion.2
  142.0 0.8 fusion.56
  (54 shorter events, 0.4 us)
Async XLA Ops:
  0.6 2.0 %copy-start = (bf16[4096,256]{1,0:T(8,128)(2,1)S(1)}, bf16[4096,256]{1,0:T(8,128)(2,1)}, u32[]{:S(2)}) copy-start(bf16[4096,256]{1,0:T(8,128)(2,1)} %param.12) | copy-start | bytes 6291460
  2.7 3.5 %copy-start.9 = (bf16[512,256]{1,0:T(8,128)(2,1)S(1)}, bf16[512,256]{1,0:T(8,128)(2,1)}, u32[]{:S(2)}) copy-start(bf16[512,256]{1,0:T(8,128)(2,1)} %param.21) | copy-start | bytes 786436
  34.3 3.2 %copy-start.2 = (bf16[512,1024]{1,0:T(8,128)(2,1)S(1)}, bf16[512,1024]{1,0:T(8,128)(2,1)}, u32[]{:S(2)}) copy-start(bf16[512,1024]{1,0:T(8,128)(2,1)} %get-tuple-element.18) | copy-start | bytes 3145732
  37.5 1.7 %copy-start.11 = (bf16[1024,256]{1,0:T(8,128)(2,1)S(1)}, bf16[1024,256]{1,0:T(8,128)(2,1)}, u32[]{:S(2)}) copy-start(bf16[1024,256]{1,0:T(8,128)(2,1)} %param.14) | copy-start | bytes 1572868
  39.2 2.6 %copy-start.3 = (bf16[512,1024]{1,0:T(8,128)(2,1)}, bf16[512,1024]{1,0:T(8,128)(2,1)S(1)}, u32[]{:S(2)}) copy-start(bf16[512,1024]{1,0:T(8,128)(2,1)S(1)} %get-tuple-element.36) | copy-start | bytes 3145732
  39.2 1.4 copy-start.6
  39.7 2.2 %copy-start.16 = (f32[9,256]{1,0:T(8,128)S(1)}, f32[9,256]{1,0:T(8,128)}, u32[]{:S(2)}) copy-start(f32[9,256]{1,0:T(8,128)} %param.15) | copy-start | bytes 27652
  40.6 10.5 %copy-start.19 = (f32[256]{0:T(256)S(1)}, f32[256]{0:T(256)}, u32[]{:S(2)}) copy-start(f32[256]{0:T(256)} %param.16) | copy-start | bytes 3076
  40.6 10.5 %copy-start.21 = (f32[256]{0:T(256)S(1)}, f32[256]{0:T(256)}, u32[]{:S(2)}) copy-start(f32[256]{0:T(256)} %param.17) | copy-start | bytes 3076
  51.1 2.9 %copy-start.13 = (f32[512,256]{1,0:T(8,128)}, f32[512,256]{1,0:T(8,128)S(1)}, u32[]{:S(2)}) copy-start(f32[512,256]{1,0:T(8,128)S(1)} %fusion.42) | copy-start | bytes 1572868
  62.3 1.9 %copy-start.5 = (f32[512,256]{1,0:T(8,128)S(1)}, f32[512,256]{1,0:T(8,128)}, u32[]{:S(2)}) copy-start(f32[512,256]{1,0:T(8,128)} %get-tuple-element.64) | copy-start | bytes 1572868
  62.4 2.1 %copy-start.17 = (f32[1,256]{1,0:T(1,128)}, f32[1,256]{1,0:T(1,128)S(1)}, u32[]{:S(2)}) copy-start(f32[1,256]{1,0:T(1,128)S(1)} %get-tuple-element.55) | copy-start | bytes 3076
  62.4 2.1 %copy-start.18 = (f32[1,256]{1,0:T(1,128)}, f32[1,256]{1,0:T(1,128)S(1)}, u32[]{:S(2)}) copy-start(f32[1,256]{1,0:T(1,128)S(1)} %get-tuple-element.56) | copy-start | bytes 3076
  62.4 2.1 %copy-start.4 = (bf16[512,1024]{1,0:T(8,128)(2,1)S(1)}, bf16[512,1024]{1,0:T(8,128)(2,1)}, u32[]{:S(2)}) copy-start(bf16[512,1024]{1,0:T(8,128)(2,1)} %copy-done.3) | copy-start | bytes 3145732
  64.5 1.0 copy-start.14
  64.5 1.4 copy-start.20
  66.5 1.3 copy-start.7
  67.8 1.6 %copy-start.1 = (f32[512,1024]{1,0:T(8,128)S(1)}, f32[512,1024]{1,0:T(8,128)}, u32[]{:S(2)}) copy-start(f32[512,1024]{1,0:T(8,128)} %get-tuple-element.37) | copy-start | bytes 6291460
  67.8 1.7 %copy-start.12 = (bf16[1024,256]{1,0:T(8,128)(2,1)S(1)}, bf16[1024,256]{1,0:T(8,128)(2,1)}, u32[]{:S(2)}) copy-start(bf16[1024,256]{1,0:T(8,128)(2,1)} %param.14) | copy-start | bytes 1572868
  137.3 3.5 %copy-start.8 = (bf16[4,512,256]{2,1,0:T(8,128)(2,1)S(1)}, bf16[4,512,256]{2,1,0:T(8,128)(2,1)}, u32[]{:S(2)}) copy-start(bf16[4,512,256]{2,1,0:T(8,128)(2,1)} %get-tuple-element.23) | copy-start | bytes 3145732
  137.3 3.7 %copy-start.15 = (bf16[8,64,256]{2,1,0:T(8,128)(2,1)S(1)}, bf16[8,64,256]{2,1,0:T(8,128)(2,1)}, u32[]{:S(2)}) copy-start(bf16[8,64,256]{2,1,0:T(8,128)(2,1)} %get-tuple-element.17) | copy-start | bytes 786436
  140.8 1.1 copy-start.10

commit v6 on v5

--- a/solution.py
+++ b/solution.py
@@ -10,6 +10,7 @@
 
 
 PIECES = 4
+AHEAD = 2
 GATHERS = ("columns", "whole", "deal")
 
 
@@ -90,8 +91,11 @@
         for hop in range(1, size // 2):
             slot = hop * pieces + piece
             peer = lax.rem(me + 2 * hop, size)
-            first = push(block, place, send.at[slot], recv.at[slot], axis, peer)
-            relays.append((piece, first, hop, (kind, axis, source, target, send, recv)))
+            start = functools.partial(
+                push, block, place, send.at[slot], recv.at[slot], axis, peer
+            )
+            first = start() if piece < AHEAD else None
+            relays.append([piece, first, hop, (kind, axis, source, target, send, recv), start])
         copies.append(push(block, place, send.at[piece], recv.at[piece], axis, partner_of(me)))
     if kind == "columns":
         width = source.shape[1]
@@ -108,19 +112,21 @@
 
 def relay_all(relays):
     copies = []
-    for piece, first, hop, (kind, axis, source, target, send, recv) in sorted(
-        relays, key=lambda relay: relay[0]
-    ):
-        size = lax.axis_size(axis)
-        me = lax.axis_index(axis)
-        pieces = pieces_of(kind, source)
-        origin = lax.rem(me + size - 2 * hop, size)
-        slot = (size // 2 + hop - 1) * pieces + piece
-        first.wait_recv()
-        place = piece_in(kind, target, source, origin, piece, pieces)
-        copies.append(push(place, place, send.at[slot], recv.at[slot], axis, partner_of(me)))
-    for _, first, _, _ in relays:
-        first.wait_send()
+    for now in range(PIECES):
+        for piece, first, hop, (kind, axis, source, target, send, recv), _ in relays:
+            if piece != now:
+                continue
+            size = lax.axis_size(axis)
+            me = lax.axis_index(axis)
+            pieces = pieces_of(kind, source)
+            origin = lax.rem(me + size - 2 * hop, size)
+            slot = (size // 2 + hop - 1) * pieces + piece
+            first.wait()
+            place = piece_in(kind, target, source, origin, piece, pieces)
+            copies.append(push(place, place, send.at[slot], recv.at[slot], axis, partner_of(me)))
+        for relay in relays:
+            if relay[0] == now + AHEAD:
+                relay[1] = relay[4]()
     return copies
 
 
@@ -145,18 +151,18 @@
     return source.at[:, pl.ds(pl.multiple_of(index * width, 128), width)]
 
 
-def start_reduce(axis, source, landing, send, recv):
+def pair_push(axis, source, landing, send, recv, step):
     half = lax.axis_size(axis) // 2
     me = lax.axis_index(axis)
+    line = lax.rem(me // 2 + 1 + step, half)
     partner = partner_of(me)
-    copies = []
-    for step in range(half):
-        line = lax.rem(me // 2 + 1 + step, half)
-        block = share_of(source, axis, 2 * line + lax.rem(partner, 2))
-        copies.append(
-            push(block, landing.at[step], send.at[step], recv.at[step], axis, partner)
-        )
-    return copies
+    block = share_of(source, axis, 2 * line + lax.rem(partner, 2))
+    return push(block, landing.at[step], send.at[step], recv.at[step], axis, partner)
+
+
+def start_reduce(axis, source, landing, send, recv):
+    first = min(AHEAD, lax.axis_size(axis) // 2)
+    return [pair_push(axis, source, landing, send, recv, step) for step in range(first)]
 
 
 def finish_reduce(axis, firsts, source, landing, partial, target, send, recv, local):
@@ -167,6 +173,8 @@
         line = lax.rem(me // 2 + 1 + step, half)
         peer = 2 * line + lax.rem(me, 2)
         firsts[step].wait()
+        if step + AHEAD < half:
+            firsts.append(pair_push(axis, source, landing, send, recv, step + AHEAD))
         mine = share_of(source, axis, peer)[...]
         both = mine.astype(jnp.float32) + landing[step].astype(jnp.float32)
         partial[step] = both.astype(partial.dtype)
@@ -249,17 +257,13 @@
 def return_kernel(
     packed,
     to_rows,
-    mixed,
     quarter,
     gathered,
-    mixed_parts,
     sub,
     landing,
     owned,
     packed_send,
     packed_recv,
-    mixed_send,
-    mixed_recv,
     owned_send,
     owned_recv,
     sub_send,
@@ -270,11 +274,9 @@
     arrivals = start_direct(
         "rows", "seq", packed, landing, packed_send, packed_recv, local_sem.at[0]
     )
-    copies = start_direct("split", "tp", mixed, mixed_parts, mixed_send, mixed_recv, local_sem.at[1])
-    sub_copies, sub_relays = start_gather(
-        "whole", "tp", quarter, sub, sub_send, sub_recv, local_sem.at[3]
-    )
-    copies += sub_copies
+    copies, sub_relays = start_gather(
+        "whole", "tp", quarter, sub, sub_send, sub_recv, local_sem.at[1]
+    )
     for copy in arrivals:
         copy.wait()
     frames = landing[...].reshape(-1, landing.shape[2])
@@ -289,7 +291,7 @@
         copy.wait()
 
 
-def send_back(number, packed, to_rows, mixed, quarter):
+def send_back(number, packed, to_rows, quarter):
     shards = lax.axis_size("seq")
     ranks = lax.axis_size("tp")
     height = to_rows.shape[0] // ranks
@@ -300,31 +302,27 @@
         return_kernel,
         out_shape=[
             jax.ShapeDtypeStruct((ranks, shards, height, width), packed.dtype),
-            jax.ShapeDtypeStruct((ranks, mixed.shape[0], mixed.shape[1] // ranks), mixed.dtype),
             jax.ShapeDtypeStruct((ranks,) + quarter.shape, quarter.dtype),
         ],
         in_specs=[
             pl.BlockSpec(memory_space=pl.ANY),
             pl.BlockSpec(memory_space=pltpu.VMEM),
             pl.BlockSpec(memory_space=pl.ANY),
-            pl.BlockSpec(memory_space=pl.ANY),
         ],
-        out_specs=[pl.BlockSpec(memory_space=pl.ANY)] * 3,
+        out_specs=[pl.BlockSpec(memory_space=pl.ANY)] * 2,
         scratch_shapes=[
             pltpu.VMEM(packed.shape, packed.dtype),
             pltpu.VMEM(owned, packed.dtype),
             dma((shards,)),
             dma((shards,)),
-            dma((ranks,)),
-            dma((ranks,)),
             dma((shards * PIECES,)),
             dma((shards * PIECES,)),
             dma((ranks * PIECES,)),
             dma((ranks * PIECES,)),
-            dma((4,)),
+            dma((3,)),
         ],
         compiler_params=pltpu.CompilerParams(collective_id=number, has_side_effects=True),
-    )(packed, to_rows, mixed, quarter)
+    )(packed, to_rows, quarter)
 
 
 def spread_kernel(
@@ -356,9 +354,6 @@
     copies, grad_relays = start_gather(
         "columns", "tp", grad_out, grad_full, grad_send, grad_recv, local_sem.at[1]
     )
-    copies += start_direct(
-        "quarter", "seq", subsampled, quarter, quarter_send, quarter_recv, local_sem.at[2]
-    )
 
     def place_of(owner, column):
         rows = pl.ds(pl.multiple_of(owner * height, 16), height)
@@ -381,6 +376,9 @@
         own = pltpu.make_async_copy(block, place, block_sem.at[step])
         own.start()
         copies.append(own)
+    copies += start_direct(
+        "quarter", "seq", subsampled, quarter, quarter_send, quarter_recv, local_sem.at[2]
+    )
     copies += relay_all(grad_relays)
     for first, owner, hop, step in firsts:
         first.wait()
@@ -569,10 +567,11 @@
         ],
         axis=1,
     )
-    normed_parts, row_parts, weight_blocks = transfer(
+    normed_parts, row_parts, mixed_parts, weight_blocks = transfer(
         5,
         ("reduce", "tp", normed_terms.astype(jnp.bfloat16)),
         ("small", "tp", row_sums),
+        ("reduce", "tp", mixed_local),
         ("reduce", "seq", weight_parts),
     )
     row_means = (summed(row_parts) / width_all).T
@@ -580,11 +579,10 @@
     grad_hidden = (summed(normed_parts) - row_means[:, 0:1] - normed_own * row_means[:, 1:2]) / sigma
     grad_packed = ((grad_out.astype(jnp.float32) + grad_hidden) * mask).astype(jnp.bfloat16)
     to_rows = (own_slots[0][:, None] == slot_ids[None, :]).astype(jnp.bfloat16)
-    grad_proj, mixed_parts, gathered_sub = send_back(
+    grad_proj, gathered_sub = send_back(
         6,
         grad_packed.reshape(shards, MOST, part_width),
         to_rows,
-        mixed_local,
         quarter.reshape(-1, quarter.shape[2]),
     )
     block_out = ((hidden_part.astype(jnp.float32) + summed(mixed_parts)) * mask).astype(

time: 144 us -> 141 us (0.979)
    pallas_call x3, Pallas kernels: 40.4 us -> 42.5 us  [transfer(): pl.pallas_call(functools.partial(transfer_kernel, plan), out_shape=outs,...]
    pallas_call x1, Pallas kernels: 31.4 us -> 29.3 us  [send_back(): pl.pallas_call(return_kernel, out_shape=[jax.ShapeDtypeStruct((ranks, sha...]
    reduce_sum x6 -> x5, other arithmetic: 3.97 us -> 3.28 us  [summed(): return jnp.sum(parts.astype(jnp.float32), axis=0)]
where the time goes in v6:
time: 141 us; the launch traced here: 140 us
  Pallas kernels  99.1 us (70%)
  other arithmetic  20.2 us (14%)
  matrix products  16.5 us (12%)
  local copies, waits for them, and re-layouts  3.54 us (3%)
    pallas_call x3, Pallas kernels, transfer(): pl.pallas_call(functools.partial(transfer_kernel, plan), out_shape=outs,...  42.5 us
    pallas_call x1, Pallas kernels, send_back(): pl.pallas_call(return_kernel, out_shape=[jax.ShapeDtypeStruct((ranks, sha...  29.3 us
    pallas_call x1, Pallas kernels, spread(): pl.pallas_call(spread_kernel, out_shape=[jax.ShapeDtypeStruct(outgoing.sh...  27.2 us
    dot_general x4, matrix products, contract_rows(): lax.dot_general(left, right, (((0,), (0,)), ((), ())), preferred_element_...  5.04 us
    dot_general x3, matrix products, contract_cols(): lax.dot_general(left, right, (((1,), (1,)), ((), ())), preferred_element_...  3.48 us
    dot_general x1, matrix products, body(): jnp.dot(to_slots, projected, preferred_element_type=jnp.float32)  3.37 us
    reduce_sum x5, other arithmetic, summed(): return jnp.sum(parts.astype(jnp.float32), axis=0)  3.28 us
    dot_general x1, matrix products, body(): jnp.dot(grad_full, down_weight, preferred_element_type=jnp.float32)  2.89 us

profile of v6, /device:TPU:0, one launch (start us, length us, event | category | flops | bytes accessed | tf_op | source)
XLA Modules:
  0.0 140.3 jit_solution(6696829978261126496)
XLA Ops:
  0.6 0.0 copy-start
  0.7 1.0 select_reduce_fusion.1
  1.7 0.8 select_reduce_fusion.2
  2.5 0.1 select_reduce_fusion
  2.7 3.4 %convolution_convert_fusion.4 = bf16[512,256]{1,0:T(8,128)(2,1)} fusion(bf16[256,4096]{1,0:T(8,128)(2,1)} %subsampled.1, bf16[4096,256]{1,0:T(8,128)(2,1)S(1)} %copy-done, s32[256]{0:T(256)S(1)} %bitcast.106), kind=kOutput, calls=%fused_computation.20 | convolution fusion | flops 604307456 | bytes 4457472 | tf_op jit(solution)/shard_map/dot_general | solution.py:504
  6.1 0.1 fusion.48
  6.1 0.1 lt.68
  6.2 0.8 broadcast_select_fusion.grad_out
  7.1 27.2 %shard_map.162 = (bf16[8,64,256]{2,1,0:T(8,128)(2,1)}, bf16[512,1024]{1,0:T(8,128)(2,1)}, bf16[512,1024]{1,0:T(8,128)(2,1)}, bf16[8,64,512]{2,1,0:T(8,128)(2,1)}) custom-call(bf16[8,64,256]{2,1,0:T(8,128)(2,1)} %bitcast.79, bf16[512,256]{1,0:T(8,128)(2,1)} %broadcast_select_fusion.grad_out, bf16[256,4096]{1,0:T(8,128)(2,1)} %subsampled.1), custom_call_target="tpu_custom_call" | custom-call | tf_op jit(solution)/shard_map/pallas_call | solution.py:401
  34.3 1.5 %convert_reduce_fusion = f32[512]{0:T(512)S(1)} fusion(bf16[512,1024]{1,0:T(8,128)(2,1)} %get-tuple-element.18), kind=kLoop, calls=%fused_computation.1 | loop fusion | flops 1048064 | bytes 1050624 | tf_op jit(solution)/shard_map/reduce_sum | solution.py:517
  35.9 1.6 %fusion.2 = f32[512]{0:T(512)S(1)} fusion(bf16[512,1024]{1,0:T(8,128)(2,1)} %get-tuple-element.18, f32[512]{0:T(512)S(1)} %broadcast_multiply_fusion.1), kind=kLoop, calls=%fused_computation.4 | loop fusion | flops 2096640 | bytes 1052672 | tf_op jit(solution)/shard_map/reduce_sum | solution.py:518
  37.5 1.7 %fusion.54 = (bf16[512,1024]{1,0:T(8,128)(2,1)S(1)}, f32[512,1024]{1,0:T(8,128)}) fusion(f32[512]{0:T(512)S(1)} %add_sqrt_fusion, f32[512]{0:T(512)S(1)} %broadcast_multiply_fusion.1, bf16[512,1024]{1,0:T(8,128)(2,1)S(1)} %copy-done.2), kind=kLoop, calls=%fused_computation.118 | loop fusion | flops 2097152 | bytes 4198400 | tf_op jit(solution)/shard_map/convert_element_type | solution.py:520
  39.2 0.5 fusion.6
  39.7 0.9 copy-done.6
  40.6 1.2 multiply_multiply_fusion.1
  41.9 0.7 multiply_reduce_fusion.3
  42.5 0.1 pad.20.clone
  42.6 0.7 maximum_maximum_fusion.1.refs_0_
  43.3 6.8 %shard_map.163 = f32[8,8,256]{2,1,0:T(8,128)} custom-call(f32[8,256]{1,0:T(8,128)} %maximum_maximum_fusion.1.refs_0_), custom_call_target="tpu_custom_call" | custom-call | tf_op jit(solution)/shard_map/pallas_call | solution.py:247
  50.1 0.9 reduce_sum.160
  51.0 0.1 fusion.42
  51.1 2.9 %fusion.50 = (f32[256]{0:T(256)S(1)}, f32[256]{0:T(256)S(1)}, f32[512,256]{1,0:T(8,128)}) fusion(f32[512,256]{1,0:T(8,128)S(1)} %fusion.42, f32[512]{0:T(512)S(1)} %convert_element_type.84, f32[256]{0:T(256)S(1)} %copy-done.21, f32[256]{0:T(256)S(1)} %copy-done.18, bf16[512,1024]{1,0:T(8,128)(2,1)} %get-tuple-element.19, bf16[1024,256]{1,0:T(8,128)(2,1)} %param.18), kind=kOutput, calls=%fused_computation.116 | convolution fusion | flops 270269952 | bytes 2627584 | tf_op jit(solution)/shard_map/dot_general | solution.py:540
  54.0 0.7 maximum_maximum_fusion.2.refs_0_
  54.7 6.8 %shard_map.164 = f32[8,8,256]{2,1,0:T(8,128)} custom-call(f32[8,256]{1,0:T(8,128)} %maximum_maximum_fusion.2.refs_0_), custom_call_target="tpu_custom_call" | custom-call | tf_op jit(solution)/shard_map/pallas_call | solution.py:247
  61.5 0.9 reduce_sum.163
  62.4 1.3 multiply_multiply_fusion
  63.7 0.5 fusion.32
  64.3 0.2 multiply_convert_fusion.2
  64.5 0.5 convolution_convert_fusion.3
  65.0 0.5 convolution_convert_fusion.2
  65.5 0.0 copy-done.13
  65.6 0.3 copy-done.19
  65.9 0.6 convolution_convert_fusion.1
  66.5 1.3 pad_maximum_fusion.refs_3_
  67.8 0.5 fusion.60
  68.2 1.1 copy-done.1
  69.4 0.1 copy-done.11
  69.5 1.5 %fusion.49 = (f32[512]{0:T(512)S(1)}, f32[512]{0:T(512)S(1)}, bf16[512,1024]{1,0:T(8,128)(2,1)}) fusion(f32[512,1024]{1,0:T(8,128)S(1)} %copy-done.1, f32[512,1024]{1,0:T(8,128)S(1)} %fusion.60, bf16[512,256]{1,0:T(8,128)(2,1)S(1)} %get-tuple-element.39, bf16[1024,256]{1,0:T(8,128)(2,1)S(1)} %copy-done.11), kind=kOutput, calls=%fused_computation.115 | convolution fusion | flops 271055872 | bytes 6033408 | tf_op jit(solution)/shard_map/dot_general | solution.py:464
  71.0 0.7 maximum_maximum_fusion.refs_1_
  71.6 1.5 %convolution_convert_fusion.refs_2_ = bf16[512,1024]{1,0:T(8,128)(2,1)} fusion(bf16[1024,256]{1,0:T(8,128)(2,1)S(1)} %copy-done.20, f32[512,256]{1,0:T(8,128)S(1)} %copy-done.13, f32[256]{0:T(256)S(1)} %copy-done.21, f32[256]{0:T(256)S(1)} %copy-done.18), kind=kOutput, calls=%fused_computation.9 | convolution fusion | flops 269877248 | bytes 2099200 | tf_op jit(solution)/shard_map/dot_general | solution.py:464
  73.1 28.9 %shard_map.165 = (bf16[2,512,256]{2,1,0:T(8,128)(2,1)}, f32[4,8,512]{2,1,0:T(8,128)}, bf16[2,512,256]{2,1,0:T(8,128)(2,1)}, bf16[4,384,256]{2,1,0:T(8,128)(2,1)}) custom-call(bf16[512,1024]{1,0:T(8,128)(2,1)} %get-tuple-element.38.refs_0_, f32[8,512]{1,0:T(8,128)} %maximum_maximum_fusion.refs_1_, bf16[512,1024]{1,0:T(8,128)(2,1)} %convolution_convert_fusion.refs_2_, ...), custom_call_target="tpu_custom_call" | custom-call | tf_op jit(solution)/shard_map/pallas_call | solution.py:247
  102.0 1.5 %convert_reduce_fusion.2 = (f32[512,256]{1,0:T(8,128)S(1)}, f32[512,256]{1,0:T(8,128)S(1)}) fusion(bf16[2,512,256]{2,1,0:T(8,128)(2,1)} %get-tuple-element.21, bf16[2,512,256]{2,1,0:T(8,128)(2,1)} %get-tuple-element.20), kind=kLoop, calls=%fused_computation.22 | loop fusion | flops 786432 | bytes 2097152 | tf_op jit(solution)/shard_map/reduce_sum | solution.py:428
  103.6 2.3 %multiply_convert_fusion = (bf16[512,256]{1,0:T(8,128)(2,1)}, bf16[512,256]{1,0:T(8,128)(2,1)}) fusion(f32[512,1024]{1,0:T(8,128)} %get-tuple-element.37, s32[]{:T(128)S(6)} %select_n.27, f32[512,256]{1,0:T(8,128)S(1)} %get-tuple-element.69, f32[512]{0:T(512)S(1)} %add_sqrt_fusion, f32[512]{0:T(512)S(1)} %bitcast.105, f32[512]{0:T(512)S(1)} %bitcast.104, ...), kind=kLoop, calls=%fused_computation.79 | loop fusion | flops 1703936 | bytes 2630148 | tf_op jit(solution)/shard_map/convert_element_type | solution.py:580
  105.9 0.8 fusion.43.to_rows
  106.7 29.3 %shard_map.166 = (bf16[4,8,64,256]{3,2,1,0:T(8,128)(2,1)}, bf16[4,512,512]{2,1,0:T(8,128)(2,1)}) custom-call(bf16[8,64,256]{2,1,0:T(8,128)(2,1)} %bitcast.74, bf16[256,512]{1,0:T(8,128)(2,1)} %fusion.43.to_rows, bf16[512,512]{1,0:T(8,128)(2,1)} %bitcast.75), custom_call_target="tpu_custom_call" | custom-call | tf_op jit(solution)/shard_map/pallas_call | solution.py:301
  136.0 3.5 %fusion.61 = f32[512,256]{1,0:T(8,128)} fusion(bf16[2048,512]{1,0:T(8,128)(2,1)} %bitcast.70, bf16[2048,256]{1,0:T(8,128)(2,1)} %bitcast.73), kind=kOutput, calls=%fused_computation.124 | convolution fusion | flops 536870912 | bytes 3670016 | tf_op jit(solution)/shard_map/dot_general | solution.py:458
  139.5 0.1 convert_reduce_fusion.1
  139.6 0.8 fusion.56
  (52 shorter events, 0.2 us)
Async XLA Ops:
  0.6 2.0 %copy-start = (bf16[4096,256]{1,0:T(8,128)(2,1)S(1)}, bf16[4096,256]{1,0:T(8,128)(2,1)}, u32[]{:S(2)}) copy-start(bf16[4096,256]{1,0:T(8,128)(2,1)} %param.12) | copy-start | bytes 6291460
  2.7 3.5 %copy-start.8 = (bf16[512,256]{1,0:T(8,128)(2,1)S(1)}, bf16[512,256]{1,0:T(8,128)(2,1)}, u32[]{:S(2)}) copy-start(bf16[512,256]{1,0:T(8,128)(2,1)} %param.21) | copy-start | bytes 786436
  34.3 3.2 %copy-start.2 = (bf16[512,1024]{1,0:T(8,128)(2,1)S(1)}, bf16[512,1024]{1,0:T(8,128)(2,1)}, u32[]{:S(2)}) copy-start(bf16[512,1024]{1,0:T(8,128)(2,1)} %get-tuple-element.18) | copy-start | bytes 3145732
  37.5 1.7 %copy-start.10 = (bf16[1024,256]{1,0:T(8,128)(2,1)S(1)}, bf16[1024,256]{1,0:T(8,128)(2,1)}, u32[]{:S(2)}) copy-start(bf16[1024,256]{1,0:T(8,128)(2,1)} %param.14) | copy-start | bytes 1572868
  39.2 2.6 %copy-start.3 = (bf16[512,1024]{1,0:T(8,128)(2,1)}, bf16[512,1024]{1,0:T(8,128)(2,1)S(1)}, u32[]{:S(2)}) copy-start(bf16[512,1024]{1,0:T(8,128)(2,1)S(1)} %get-tuple-element.36) | copy-start | bytes 3145732
  39.2 1.4 copy-start.6
  39.7 2.2 %copy-start.15 = (f32[9,256]{1,0:T(8,128)S(1)}, f32[9,256]{1,0:T(8,128)}, u32[]{:S(2)}) copy-start(f32[9,256]{1,0:T(8,128)} %param.15) | copy-start | bytes 27652
  40.6 10.5 %copy-start.18 = (f32[256]{0:T(256)S(1)}, f32[256]{0:T(256)}, u32[]{:S(2)}) copy-start(f32[256]{0:T(256)} %param.16) | copy-start | bytes 3076
  40.6 10.5 %copy-start.21 = (f32[256]{0:T(256)S(1)}, f32[256]{0:T(256)}, u32[]{:S(2)}) copy-start(f32[256]{0:T(256)} %param.17) | copy-start | bytes 3076
  51.1 2.9 %copy-start.12 = (f32[512,256]{1,0:T(8,128)}, f32[512,256]{1,0:T(8,128)S(1)}, u32[]{:S(2)}) copy-start(f32[512,256]{1,0:T(8,128)S(1)} %fusion.42) | copy-start | bytes 1572868
  62.4 1.9 %copy-start.5 = (f32[512,256]{1,0:T(8,128)S(1)}, f32[512,256]{1,0:T(8,128)}, u32[]{:S(2)}) copy-start(f32[512,256]{1,0:T(8,128)} %get-tuple-element.66) | copy-start | bytes 1572868
  62.4 2.1 %copy-start.16 = (f32[1,256]{1,0:T(1,128)}, f32[1,256]{1,0:T(1,128)S(1)}, u32[]{:S(2)}) copy-start(f32[1,256]{1,0:T(1,128)S(1)} %get-tuple-element.55) | copy-start | bytes 3076
  62.4 2.1 %copy-start.17 = (f32[1,256]{1,0:T(1,128)}, f32[1,256]{1,0:T(1,128)S(1)}, u32[]{:S(2)}) copy-start(f32[1,256]{1,0:T(1,128)S(1)} %get-tuple-element.56) | copy-start | bytes 3076
  62.4 2.1 %copy-start.4 = (bf16[512,1024]{1,0:T(8,128)(2,1)S(1)}, bf16[512,1024]{1,0:T(8,128)(2,1)}, u32[]{:S(2)}) copy-start(bf16[512,1024]{1,0:T(8,128)(2,1)} %copy-done.3) | copy-start | bytes 3145732
  64.5 1.0 copy-start.13
  64.5 1.4 copy-start.19
  66.5 1.3 copy-start.7
  67.8 1.6 %copy-start.1 = (f32[512,1024]{1,0:T(8,128)S(1)}, f32[512,1024]{1,0:T(8,128)}, u32[]{:S(2)}) copy-start(f32[512,1024]{1,0:T(8,128)} %get-tuple-element.37) | copy-start | bytes 6291460
  67.8 1.7 %copy-start.11 = (bf16[1024,256]{1,0:T(8,128)(2,1)S(1)}, bf16[1024,256]{1,0:T(8,128)(2,1)}, u32[]{:S(2)}) copy-start(bf16[1024,256]{1,0:T(8,128)(2,1)} %param.14) | copy-start | bytes 1572868
  69.5 2.2 %copy-start.20 = (bf16[1024,256]{1,0:T(8,128)(2,1)S(1)}, bf16[1024,256]{1,0:T(8,128)(2,1)}, u32[]{:S(2)}) copy-start(bf16[1024,256]{1,0:T(8,128)(2,1)} %param.18) | copy-start | bytes 1572868
  102.0 1.5 %copy-start.14 = (f32[4,8,512]{2,1,0:T(8,128)S(1)}, f32[4,8,512]{2,1,0:T(8,128)}, u32[]{:S(2)}) copy-start(f32[4,8,512]{2,1,0:T(8,128)} %get-tuple-element.22) | copy-start | bytes 196612
  136.0 3.5 %copy-start.9 = (bf16[4,384,256]{2,1,0:T(8,128)(2,1)S(1)}, bf16[4,384,256]{2,1,0:T(8,128)(2,1)}, u32[]{:S(2)}) copy-start(bf16[4,384,256]{2,1,0:T(8,128)(2,1)} %get-tuple-element.26) | copy-start | bytes 2359300
